TPU v7x, 32 devices: a whole 2x2x4 slice. The times are simulated.
32 devices in a mesh: line: 8 (over y, x, core), col: 4 (over z).
Axes of the slice: x: 2, y: 2, z: 4, core: 2. Of those that a mesh axis runs over, the one named last changes fastest.
Arguments:
- fields: float32 [4, 256, 32, 512], P(None, 'line', 'col'), may hold values from -4 to 4
- viscosity: float32 [256, 32, 512], P('line', 'col'), may hold values from 0.5 to 2
Outputs:
- updated: float32 [4, 256, 32, 512], P(None, 'line', 'col')
All inputs are finite; a program needn't handle non-finite values.
Results may differ from a plain program's by a relative error of at most 0.0003.
Values sent between devices are 32-bit elements; how exact they have to be, the bound alone decides.
No kernel may reach another device: no remote copies, remote signals or barrier semaphores. Data moves between devices by JAX's collectives and lax.ppermute only.
A program may use at most 64 MiB of HBM per device.

v0:
```python
import functools

import jax
import jax.numpy as jnp
from jax import lax
from jax.experimental import pallas as pl
from jax.experimental.pallas import tpu as pltpu
from jax.sharding import PartitionSpec as P

STIFF = 3072
THERMAL_RATIO = 0.8
CROSS_RATE = 0.2
ADVECTION = 0.25
BUOYANCY = 2.0
SCALES = (1.0, THERMAL_RATIO)
KIND = (0, 0, 0, 1)

F32 = jnp.float32
VMEM = pltpu.VMEM
LIMIT = 24 * 1024 * 1024

G00, G0N, GNN = (0, 3), (1, 4), (2, 5)
V_FIRST, V_LAST, F_FIRST, F_LAST = 6, 7, 8, 12
PLANES = 16
R_, GA, GB, CA, CB = 0, 2, 4, 6, 10
JOINT = 14


def in_vmem(x):
    return pltpu.with_memory_space_constraint(x, VMEM)


def spec():
    return pl.BlockSpec(memory_space=VMEM)


def call(kernel, name, out_shapes, args, scratch=(), in_hbm=(), out_hbm=(), aliases={}, flops=0, moved=0):
    in_specs = []
    operands = []
    for i, x in enumerate(args):
        if i in in_hbm:
            in_specs.append(pl.BlockSpec(memory_space=pltpu.HBM))
            operands.append(pltpu.with_memory_space_constraint(x, pltpu.HBM))
        else:
            in_specs.append(spec())
            operands.append(in_vmem(x))
    out_shape = []
    out_specs = []
    for i, s in enumerate(out_shapes):
        if i in out_hbm:
            out_shape.append(pltpu.HBM(s, F32))
            out_specs.append(pl.BlockSpec(memory_space=pltpu.HBM))
        else:
            out_shape.append(VMEM(s, F32))
            out_specs.append(spec())
    return pl.pallas_call(
        kernel,
        out_shape=out_shape,
        in_specs=in_specs,
        out_specs=out_specs,
        scratch_shapes=list(scratch),
        input_output_aliases=aliases,
        compiler_params=pltpu.CompilerParams(vmem_limit_bytes=LIMIT),
        cost_estimate=pl.CostEstimate(flops=flops, bytes_accessed=moved, transcendentals=0),
        name=name,
    )(*operands)


def layer(read, ny, nz):
    sub = lax.broadcasted_iota(jnp.int32, (8, nz), 0)
    tile = jnp.broadcast_to(read(0), (8, nz))
    for r in range(1, 8):
        tile = jnp.where(sub == r, jnp.broadcast_to(read(r), (8, nz)), tile)
    return tile


def cut_kernel(at, fields, visc, *refs):
    out, sems = refs[-2:]
    copies = [pltpu.make_async_copy(fields.at[k, :, at], out.at[k], sems.at[k]) for k in range(4)]
    copies.append(pltpu.make_async_copy(visc.at[:, at], out.at[4], sems.at[4]))
    for copy in copies:
        copy.start()
    for copy in copies:
        copy.wait()


def factor_kernel(rows, fields_ref, visc, inv, cpr, g0, gn, w, tau, sems):
    copies = [
        pltpu.make_async_copy(fields_ref.at[:, 0], w.at[F_FIRST : F_FIRST + 4], sems.at[0]),
        pltpu.make_async_copy(fields_ref.at[:, rows - 1], w.at[F_LAST : F_LAST + 4], sems.at[1]),
    ]
    for copy in copies:
        copy.start()
    ny, nz = visc.shape[1], visc.shape[2]
    me = lax.axis_index("line")
    wall_low = jnp.where(me == 0, 1.0, 0.0).astype(F32)
    wall_high = jnp.where(me == lax.axis_size("line") - 1, 1.0, 0.0).astype(F32)
    one = jnp.ones((ny, nz), F32)

    def row(i, carry):
        low, v = carry[4], carry[5]
        after = visc[jnp.minimum(i + 1, rows - 1)]
        high = jnp.where(i == rows - 1, (0.5 * STIFF) * wall_high * v, (0.5 * STIFF) * (v + after))
        new = []
        for s in range(2):
            gain, running = carry[2 * s], carry[2 * s + 1]
            down = SCALES[s] * low if s else low
            up = SCALES[s] * high if s else high
            q = 1.0 + down * gain
            one_over = 1.0 / (q + up)
            coupling = up * one_over
            inv[s, i] = one_over
            cpr[s, i] = coupling
            tau[s, i] = running
            new += [q * one_over, coupling * running]
        return tuple(new) + (high, after)

    first = visc[0]
    lax.fori_loop(0, rows, row, (one,) * 4 + (wall_low * (0.5 * STIFF) * first, first))

    end = rows - 1
    start = []
    for s in range(2):
        a = inv[s, end] * tau[s, end]
        b = inv[s, end]
        g0[s, end] = a
        gn[s, end] = b
        w[G0N[s]] = a
        w[GNN[s]] = b
        start += [a, b]

    def back(j, carry):
        i = end - 1 - j
        new = []
        for s in range(2):
            c = cpr[s, i]
            a = inv[s, i] * tau[s, i] + c * carry[2 * s]
            b = c * carry[2 * s + 1]
            g0[s, i] = a
            gn[s, i] = b
            new += [a, b]
        return tuple(new)

    final = lax.fori_loop(0, end, back, tuple(start))
    for s in range(2):
        w[G00[s]] = final[2 * s]
    w[V_FIRST] = first
    w[V_LAST] = visc[rows - 1]
    for copy in copies:
        copy.wait()


def explicit_rows(first, count, base, start, fields, visc, src):
    rows, ny, nz = visc.shape
    lane = lax.broadcasted_iota(jnp.int32, (ny, nz), 1)
    sub = lax.broadcasted_iota(jnp.int32, (ny, nz), 0)
    z_top, z_low = lane == nz - 1, lane == 0
    y_top, y_low = sub == ny - 1, sub == 0

    def sides(x):
        return (
            pltpu.roll(x, ny - 1, 0),
            pltpu.roll(x, 1, 0),
            pltpu.roll(x, nz - 1, 1),
            pltpu.roll(x, 1, 1),
        )

    def row(i, _):
        f = [fields[k, i - base] for k in range(4)]
        v = visc[i]
        after, before = jnp.minimum(i + 1, rows - 1), jnp.maximum(i - 1, 0)
        vyn, vyp, vzn, vzp = sides(v)
        half = 0.5 * CROSS_RATE
        faces = [
            jnp.where(y_top, 0.0, half * (v + vyn)),
            jnp.where(y_low, 0.0, half * (v + vyp)),
            half * (v + jnp.where(z_top, 0.0, vzn)),
            half * (v + jnp.where(z_low, 0.0, vzp)),
        ]
        none = [y_top, y_low, z_top, z_low]
        total = (faces[0] + faces[1]) + (faces[2] + faces[3])
        adv = [(-0.5 * ADVECTION) * f[k] for k in range(3)]
        move = [adv[1], -adv[1], adv[2], -adv[2]]
        adv_after = jnp.where(i == rows - 1, 0.0, adv[0])
        adv_before = jnp.where(i == 0, 0.0, adv[0])
        weights, centre = [], []
        for s in range(2):
            scaled = [SCALES[s] * x if s else x for x in faces]
            weights.append([jnp.where(n, 0.0, x + m) for n, x, m in zip(none, scaled, move)])
            centre.append(1.0 - (SCALES[s] * total if s else total))
        for k in range(4):
            s = KIND[k]
            near = sides(f[k])
            out = centre[s] * f[k] + adv_after * fields[k, after - base] - adv_before * fields[k, before - base]
            for c, x in zip(weights[s], near):
                out = out + c * x
            if k == 2:
                out = out + BUOYANCY * f[3]
            src[k, i - start] = out
        return 0

    lax.fori_loop(first, first + count, row, 0)


def early_kernel(count, fields_ref, visc, src, fields, sem):
    copy = pltpu.make_async_copy(fields_ref.at[:, 0 : count + 1], fields, sem)
    copy.start()
    copy.wait()
    explicit_rows(0, count, 0, 0, fields, visc, src)


def explicit_kernel(count, fields_ref, visc, g0, gn, early, src, p, ends, fields, sems):
    rows, ny, nz = visc.shape
    cuts = [count - 1] + list(range(2 * count + 1, rows, count)) + [rows]
    copies = []
    for c, (lo, hi) in enumerate(zip(cuts, cuts[1:])):
        copies.append(
            pltpu.make_async_copy(
                fields_ref.at[:, lo:hi], fields.at[:, lo - cuts[0] : hi - cuts[0]], sems.at[c]
            )
        )
        copies[-1].start()
    for c, copy in enumerate(copies):
        copy.wait()
        explicit_rows((c + 1) * count, count, cuts[0], count, fields, visc, src)

    def dot(ref, shift):
        def add(i, carry):
            new = []
            for g, base in ((g0, 0), (gn, 4)):
                for k in range(4):
                    new.append(carry[base + k] + g[KIND[k], i] * ref[k, i - shift])
            return tuple(new)

        return add

    final = (jnp.zeros((ny, nz), F32),) * 8
    final = lax.fori_loop(0, count, dot(early, 0), final)
    final = lax.fori_loop(count, rows, dot(src, count), final)
    for k in range(8):
        p[k] = final[k]

    for s in range(2):
        for side, at in ((0, 0), (1, ny - 1)):
            for which, g in ((0, g0), (1, gn)):
                for lo in range(0, rows, 8):
                    ends[4 * side + 2 * which + s, lo : lo + 8] = layer(
                        lambda r: g[s, lo + r, at : at + 1, :], ny, nz
                    )


def edge_kernel(rows, ny, y_last, y_first, low, high, ends, p, *refs):
    add, out = refs[-2:]
    nz = out.shape[2]
    sub = lax.broadcasted_iota(jnp.int32, (ny, 128), 0)
    rate = 0.5 * ADVECTION
    for j in range(nz // 128):
        z = pl.ds(j * 128, 128)
        sums = []
        for side, mine, far, sign in ((0, y_first, low, rate), (4, y_last, high, -rate)):
            total = [None] * 8
            for r in range(rows // 8):
                x = pl.ds(r * 8, 8)
                face = (0.5 * CROSS_RATE) * (mine[4, x, z] + far[4, x, z])
                faces = (face, THERMAL_RATIO * face)
                adv = sign * mine[1, x, z]
                both = [adv + c for c in faces]
                g = [ends[side + q, x, z] for q in range(4)]
                for k in range(4):
                    s = KIND[k]
                    h = both[s] * far[k, x, z] - faces[s] * mine[k, x, z]
                    add[side + k, x, z] = h
                    for slot, c in ((k, g[s]), (4 + k, g[2 + s])):
                        part = c * h
                        total[slot] = part if total[slot] is None else total[slot] + part
            sums.append(total)
        for slot in range(8):
            add_low = jnp.sum(sums[0][slot], axis=0, keepdims=True)
            add_high = jnp.sum(sums[1][slot], axis=0, keepdims=True)
            both = jnp.where(sub == 0, add_low, jnp.where(sub == ny - 1, add_high, 0.0))
            out[slot, :, z] = p[slot, :, z] + both


def side_bit(level):
    return jnp.bitwise_and(jnp.right_shift(lax.axis_index("line"), level), 1) == 0


def join(left, right):
    face = left[V_LAST] + right[V_FIRST]
    joint, new, ratio = {}, {}, []
    for s in range(2):
        resist = 1.0 / ((0.5 * STIFF * SCALES[s]) * face)
        r = 1.0 / (resist + left[GNN[s]] + right[G00[s]])
        ratio.append(r)
        a, b = left[G0N[s]], right[G0N[s]]
        joint[R_ + s] = r
        joint[GA + s] = a
        joint[GB + s] = b
        new[G00[s]] = left[G00[s]] - r * a * a
        new[GNN[s]] = right[GNN[s]] - r * b * b
        new[G0N[s]] = r * a * b
    rate = 0.5 * ADVECTION
    for k in range(4):
        s = KIND[k]
        add_a = -rate * left[F_LAST] * right[F_FIRST + k]
        add_b = rate * right[F_FIRST] * left[F_LAST + k]
        e = ratio[s] * (left[GNN[s]] * add_a - right[G00[s]] * add_b)
        joint[CA + k] = add_a - e
        joint[CB + k] = add_b + e
        new[F_FIRST + k] = left[F_FIRST + k]
        new[F_LAST + k] = right[F_LAST + k]
    new[V_FIRST] = left[V_FIRST]
    new[V_LAST] = right[V_LAST]
    return joint, new


def sided(low_side, mine, theirs):
    left = {p: jnp.where(low_side, mine[p], theirs[p]) for p in mine}
    right = {p: jnp.where(low_side, theirs[p], mine[p]) for p in mine}
    return left, right


def pair_kernel(own, other, *refs):
    joint, out = refs[-2:]
    low_side = side_bit(0)
    planes = range(PLANES)
    found, new = join(*sided(low_side, {p: own[p] for p in planes}, {p: other[p] for p in planes}))
    for plane in range(JOINT):
        joint[plane] = found[plane]
    width = out.shape[2]
    for plane in planes:
        out[plane] = jnp.where(low_side, new[plane][:, :width], new[plane][:, width:])


def chips_kernel(levels, own, *refs):
    others = refs[: 2 ** (levels - 1) - 1]
    joints = refs[-(2 * levels - 3) : len(refs) - (levels - 2)]
    consts = refs[len(refs) - (levels - 2) :]
    blocks = [{p: x[p] for p in range(PLANES)} for x in (own, *others)]
    zero = jnp.zeros_like(own[0])
    ends = [{p: zero for p in range(8)} for _ in blocks]
    for level in range(1, levels):
        low_side = side_bit(level)
        joined, new_ends = [], []
        for j in range(0, len(blocks), 2):
            found, new = join(*sided(low_side, blocks[j], blocks[j + 1]))
            for plane in range(JOINT):
                joints[level - 1][j // 2, plane] = found[plane]
            joined.append(new)
            if level < levels - 1:
                left, right = sided(low_side, ends[j], ends[j + 1])
                both = {}
                for k in range(4):
                    _, both[k], both[4 + k] = up(found, k, left, right)
                new_ends.append(both)
        blocks, ends = joined, new_ends
        if level < levels - 1:
            for slot, x in enumerate(facing(level + 1, levels, ends[1], False)):
                consts[level - 1][slot] = x


def facing(level, levels, ends, mine):
    if level < levels - 1:
        return [ends[p] for p in range(8)]
    low_side = side_bit(level)
    if not mine:
        low_side = jnp.logical_not(low_side)
    return [jnp.where(low_side, ends[4 + k], ends[k]) for k in range(4)]


def source_kernel(rows, count, early, src, cpr, add, t):
    ny, nz = src.shape[2], src.shape[3]
    sub = lax.broadcasted_iota(jnp.int32, (ny, nz), 0)
    top, low = sub == ny - 1, sub == 0

    def down(ref, shift):
        def row(i, carry):
            prev = jnp.maximum(i - 1, 0)
            new = []
            for k in range(4):
                a = jnp.broadcast_to(add[k, pl.ds(i, 1), :], (ny, nz))
                b = jnp.broadcast_to(add[4 + k, pl.ds(i, 1), :], (ny, nz))
                x = ref[k, i - shift] + jnp.where(low, a, jnp.where(top, b, 0.0))
                x = x + cpr[KIND[k], prev] * carry[k]
                t[k, i] = x
                new.append(x)
            return tuple(new)

        return row

    state = (jnp.zeros((ny, nz), F32),) * 4
    state = lax.fori_loop(0, count, down(early, 0), state)
    lax.fori_loop(count, rows, down(src, count), state)


def back_kernel(rows, t, inv, cpr, part):
    end = rows - 1
    start = []
    for k in range(4):
        x = inv[KIND[k], end] * t[k, end]
        part[k, end] = x
        start.append(x)

    def row(j, carry):
        i = end - 1 - j
        new = []
        for k in range(4):
            s = KIND[k]
            x = inv[s, i] * t[k, i] + cpr[s, i] * carry[k]
            part[k, i] = x
            new.append(x)
        return tuple(new)

    lax.fori_loop(0, end, row, tuple(start))


def up(joint, k, left, right):
    s = KIND[k]
    d = left[4 + k] - right[k]
    flow = joint[R_ + s] * d
    first = left[k] + joint[GA + s] * (joint[CA + k] - flow)
    last = right[4 + k] + joint[GB + s] * (joint[CB + k] + flow)
    return d, first, last


def up_kernel(levels, own, other, joint, *refs):
    joints = refs[: levels - 1]
    out, diff = refs[levels : levels + 2]
    shares = refs[levels + 2 :]
    low_side = side_bit(0)
    width = out.shape[2]
    left, right = sided(low_side, {p: own[p] for p in range(8)}, {p: other[p] for p in range(8)})
    ends = {}
    for k in range(4):
        diff[k], first, last = up(joint, k, left, right)
        ends[k] = jnp.where(low_side, first[:, :width], first[:, width:])
        ends[4 + k] = jnp.where(low_side, last[:, :width], last[:, width:])
        out[k] = ends[k]
        out[4 + k] = ends[4 + k]
    for level in range(1, levels - 1):
        low_side = side_bit(level)
        joint = joints[level - 1].at[0]
        for k in range(4):
            s = KIND[k]
            first, last = ends[k], ends[4 + k]
            flow = joint[R_ + s] * jnp.where(low_side, last, -first)
            ends[k] = jnp.where(low_side, first, 0.0) - joint[GA + s] * flow
            ends[4 + k] = jnp.where(low_side, 0.0, last) + joint[GB + s] * flow
        for slot, x in enumerate(facing(level + 1, levels, ends, True)):
            shares[level - 1][slot] = x


def joint_flow(joint, k, d, into_first, into_last, low_side):
    s = KIND[k]
    flow = joint[R_ + s] * (d + joint[GA + s] * into_first - joint[GB + s] * into_last)
    first = jnp.where(low_side, into_first, joint[CB + k] + flow)
    last = jnp.where(low_side, joint[CA + k] - flow, into_last)
    return first, last


def beside_kernel(levels, *refs):
    parts, refs = list(refs[: 2 ** (levels - 1) - levels]), refs[2 ** (levels - 1) - levels :]
    consts, outs = refs[: levels - 2], refs[levels - 2 :]
    for level in range(2, levels):
        here = [parts.pop(0) for _ in range(2 ** (level - 1) - 1)]
        for p in range(outs[level - 2].shape[0]):
            total = consts[level - 2][p]
            for part in here:
                total = total + part[p]
            outs[level - 2][p] = total


def settle_kernel(levels, own, *refs):
    near, refs = refs[: levels - 1], refs[levels - 1 :]
    far, joints, out = refs[: levels - 2], refs[levels - 2 : -1], refs[-1]
    ends = {p: own[p] for p in range(8)}
    diffs = []
    for level in range(1, levels):
        low_side = side_bit(level)
        beside = {p: near[level - 1][p] for p in range(near[level - 1].shape[0])}
        if level > 1:
            beside = {p: x + far[level - 2][p] for p, x in beside.items()}
        across = []
        if len(beside) == 4:
            for k in range(4):
                x = beside[k]
                across.append(jnp.where(low_side, ends[4 + k] - x, x - ends[k]))
        else:
            left, right = sided(low_side, ends, beside)
            for k in range(4):
                d, ends[k], ends[4 + k] = up(joints[level - 1].at[0], k, left, right)
                across.append(d)
        diffs.append(across)
    for k in range(4):
        first = last = jnp.zeros_like(diffs[0][0])
        for level in range(levels - 1, 0, -1):
            first, last = joint_flow(
                joints[level - 1].at[0], k, diffs[level - 1][k], first, last, side_bit(level)
            )
        out[k] = first
        out[4 + k] = last


def final_kernel(mine, parts, flux, joint, diff, part, g0, gn, *refs):
    out, buf, sems = refs[-3:]
    rows, half = buf.shape[1], buf.shape[3]
    low_side = side_bit(0)
    core = jnp.bitwise_and(lax.axis_index("line"), 1)
    offset = (core if mine else 1 - core) * half
    copies = []
    for c in range(half // 128):
        near = pl.ds(c * 128, 128)
        z = pl.ds(pl.multiple_of(offset + c * 128, 128), 128)
        across = {plane: joint[plane, :, z] for plane in range(JOINT)}
        into = [
            joint_flow(across, k, diff[k, :, z], flux[k, :, near], flux[4 + k, :, near], low_side)
            for k in range(4)
        ]
        for r in range(parts):
            x = pl.ds(r * (rows // parts), rows // parts)
            for i in range(x.start, x.start + x.size):
                a = [g0[s, i, :, z] for s in range(2)]
                b = [gn[s, i, :, z] for s in range(2)]
                for k in range(4):
                    s = KIND[k]
                    buf[k, i, :, near] = part[k, i, :, z] + (a[s] * into[k][0] + b[s] * into[k][1])
            copies.append(
                pltpu.make_async_copy(
                    buf.at[:, x, :, near], out.at[:, x, :, z], sems.at[c * parts + r]
                )
            )
            copies[-1].start()
    for copy in copies:
        copy.wait()


def local(fields, viscosity):
    rows, ny, nz = viscosity.shape
    lines = lax.axis_size("line")
    cols = lax.axis_size("col")
    levels = lines.bit_length() - 1
    half = nz // 2
    cells = rows * ny * nz
    block = (rows, ny, nz)

    ring = [(i, (i + 1) % cols) for i in range(cols)]
    back_ring = [(b, a) for a, b in ring]

    def gather(at_level):
        found = {}
        for d in sorted(range(1, lines // 2), key=lambda d: (-d.bit_count(), d)):
            x = at_level[d.bit_length()]
            found[d] = lax.ppermute(x, "line", [(i, i ^ (d << 1)) for i in range(lines)])
        return [found[d] for d in sorted(found)]

    def swap(x, level):
        return lax.ppermute(x, "line", [(i, i ^ (1 << level)) for i in range(lines)])

    def cut(at, name, order, flops):
        return call(
            functools.partial(cut_kernel, at),
            name,
            [(5, rows, nz)],
            [fields, viscosity] + order,
            scratch=[pltpu.SemaphoreType.DMA((5,))],
            in_hbm=(0, 1),
            flops=flops,
        )[0]

    y_last = cut(ny - 1, "cut_last", [], 5 * 10**8)
    low = lax.ppermute(y_last, "col", ring)
    y_first = cut(0, "cut_first", [y_last], 5 * 10**8)
    high = lax.ppermute(y_first, "col", back_ring)

    inv, cpr, g0, gn, w = call(
        functools.partial(factor_kernel, rows),
        "factor",
        [(2,) + block] * 4 + [(PLANES, ny, nz)],
        [fields, viscosity],
        scratch=[VMEM((2,) + block, F32), pltpu.SemaphoreType.DMA((2,))],
        in_hbm=(0,),
        flops=10**9,
    )
    count = rows // 4
    (early,) = call(
        functools.partial(early_kernel, count),
        "early",
        [(4, count, ny, nz)],
        [fields, viscosity],
        scratch=[VMEM((4, count + 1, ny, nz), F32), pltpu.SemaphoreType.DMA],
        in_hbm=(0,),
        flops=4 * 10**9,
    )
    src, p, ends = call(
        functools.partial(explicit_kernel, count),
        "explicit",
        [(4, rows - count, ny, nz), (8, ny, nz), (8, rows, nz)],
        [fields, viscosity, g0, gn, early],
        scratch=[VMEM((4, rows - count + 1, ny, nz), F32), pltpu.SemaphoreType.DMA((3,))],
        in_hbm=(0,),
        flops=5 * 10**9,
    )
    pair, w = call(
        pair_kernel,
        "pair",
        [(JOINT, ny, nz), (PLANES, ny, half)],
        [w, swap(w, 0), early],
        moved=4 * ny * nz * 60,
    )
    pairs = lines // 2
    widths = [8] * (levels - 3) + [4]
    found = call(
        functools.partial(chips_kernel, levels),
        "chips",
        [(pairs >> level, JOINT, ny, half) for level in range(1, levels)]
        + [(width, ny, half) for width in widths],
        [w] + gather([w] * (levels + 1)) + [p],
        moved=4 * ny * half * 300,
    )
    joints, consts = list(found[: levels - 1]), list(found[levels - 1 :])

    add, p = call(
        functools.partial(edge_kernel, rows, ny),
        "edge",
        [(8, rows, nz), (8, ny, nz)],
        [y_last, y_first, low, high, ends, p, joints[0]],
        flops=5 * 10**8,
    )
    (t,) = call(
        functools.partial(source_kernel, rows, count),
        "source",
        [(4,) + block],
        [early, src, cpr, add],
        flops=30 * cells,
        moved=24 * cells,
    )
    (part,) = call(
        functools.partial(back_kernel, rows),
        "back",
        [(4,) + block],
        [t, inv, cpr],
        flops=20 * cells,
        moved=24 * cells,
    )
    p, diff, *shares = call(
        functools.partial(up_kernel, levels),
        "up",
        [(8, ny, half), (4, ny, nz)] + [(width, ny, half) for width in widths],
        [p, swap(p, 0), pair] + joints + [part],
        moved=4 * ny * nz * 40,
    )
    others = dict(enumerate(gather([None, p] + shares), 1))
    near = [others.pop(1 << level) for level in range(levels - 1)]
    beside = call(
        functools.partial(beside_kernel, levels),
        "beside",
        [(width, ny, half) for width in widths],
        list(others.values()) + consts,
        flops=6 * 10**8,
    )
    (flux,) = call(
        functools.partial(settle_kernel, levels),
        "settle",
        [(8, ny, half)],
        [p] + near + list(beside) + joints,
        moved=4 * ny * half * 100,
    )
    rest = [pair, diff, part, g0, gn]
    parts = 4 if rows % 4 == 0 else 1
    scratch = [VMEM((4, rows, ny, half), F32), pltpu.SemaphoreType.DMA((half // 128 * parts,))]
    (out,) = call(
        functools.partial(final_kernel, True, parts),
        "final_own",
        [(4,) + block],
        [flux] + rest,
        scratch=scratch,
        out_hbm=(0,),
        flops=10**9,
    )
    (out,) = call(
        functools.partial(final_kernel, False, parts),
        "final_other",
        [(4,) + block],
        [swap(flux, 0)] + rest + [out],
        scratch=scratch,
        in_hbm=(6,),
        out_hbm=(0,),
        aliases={6: 0},
        flops=10**9,
    )
    return out


def solution(mesh):
    return jax.shard_map(
        local,
        mesh=mesh,
        in_specs=(P(None, "line", "col", None), P("line", "col", None)),
        out_specs=P(None, "line", "col", None),
        check_vma=False,
    )
```

profile of v0, /device:TPU:0, one launch (start us, length us, event | category | flops | bytes accessed | tf_op | source)
XLA Modules:
  0.0 32.1 jit_solution(2447095599257477749)
XLA Ops:
  0.0 1.1 %cut_last.1.refs_0_.y_last = f32[5,32,512]{2,1,0:T(8,128)S(1)} custom-call(f32[4,32,8,512]{3,2,1,0:T(8,128)} %fields_ref.5, f32[32,8,512]{2,1,0:T(8,128)} %visc.9), custom_call_target="tpu_custom_call" | custom-call | flops 500000000 | tf_op jit(solution)/shard_map/cut_last/pallas_call | solution.py:56
  1.1 3.1 %collective-permute-start = (f32[5,32,512]{2,1,0:T(8,128)S(1)}, f32[5,32,512]{2,1,0:T(8,128)S(1)}, u32[]{:S(2)}, u32[]{:S(2)}) collective-permute-start(f32[5,32,512]{2,1,0:T(8,128)S(1)} %cut_last.1.refs_0_.y_last), channel_id=1, source_target_pairs={{0,1},{1,2},{2,3},{3,0},{4,5},{5,6},{6,7},{7,4},{8,9},{9,10},{10,1... | collective-permute-start | bytes 983048 | tf_op jit(solution)/shard_map/ppermute | solution.py:571
  4.2 1.1 %cut_first.1.y_first = f32[5,32,512]{2,1,0:T(8,128)S(1)} custom-call(f32[4,32,8,512]{3,2,1,0:T(8,128)} %fields_ref.5, f32[32,8,512]{2,1,0:T(8,128)} %visc.9, f32[5,32,512]{2,1,0:T(8,128)S(1)} %cut_last.1.refs_0_.y_last), custom_call_target="tpu_custom_call" | custom-call | flops 500000000 | tf_op jit(solution)/shard_map/cut_first/pallas_call | solution.py:56
  5.2 2.1 %collective-permute-start.1 = (f32[5,32,512]{2,1,0:T(8,128)S(1)}, f32[5,32,512]{2,1,0:T(8,128)S(1)}, u32[]{:S(2)}, u32[]{:S(2)}) collective-permute-start(f32[5,32,512]{2,1,0:T(8,128)S(1)} %cut_first.1.y_first), channel_id=1, source_target_pairs={{1,0},{2,1},{3,2},{0,3},{5,4},{6,5},{7,6},{4,7},{9,8},{10,9},{11,1... | collective-permute-start | bytes 983048 | tf_op jit(solution)/shard_map/ppermute | solution.py:573
  7.4 0.9 %factor.1 = (f32[2,32,8,512]{3,2,1,0:T(8,128)S(1)}, f32[2,32,8,512]{3,2,1,0:T(8,128)S(1)}, f32[2,32,8,512]{3,2,1,0:T(8,128)S(1)}, f32[2,32,8,512]{3,2,1,0:T(8,128)S(1)}, f32[16,8,512]{2,1,0:T(8,128)S(1)}) custom-call(f32[4,32,8,512]{3,2,1,0:T(8,128)} %fields_ref.5, f32[32,8,512]{2,1,0:T(8,128)S(1)} %copy-done), custom_call_target="tpu_custom_call" | custom-call | flops 1000000000 | tf_op jit(solution)/shard_map/factor/pallas_call | solution.py:56
  8.4 2.0 %early.1.refs_0_ = f32[4,8,8,512]{3,2,1,0:T(8,128)S(1)} custom-call(f32[4,32,8,512]{3,2,1,0:T(8,128)} %fields_ref.5, f32[32,8,512]{2,1,0:T(8,128)S(1)} %copy-done), custom_call_target="tpu_custom_call" | custom-call | flops 4000000000 | tf_op jit(solution)/shard_map/early/pallas_call | solution.py:56
  10.5 2.7 %collective-permute-start.5 = (f32[16,8,256]{2,1,0:T(8,128)S(1)}, f32[16,8,256]{2,1,0:T(8,128)S(1)}, u32[]{:S(2)}, u32[]{:S(2)}) collective-permute-start(f32[16,8,256]{2,1,0:T(8,128)S(1)} %get-tuple-element.28.own), channel_id=1, source_target_pairs={{0,24},{4,28},{8,16},{12,20},{16,8},{20,12},{24,0},{28,4},{1,25},{... | collective-permute-start | bytes 393224 | tf_op jit(solution)/shard_map/ppermute | solution.py:553
  13.2 0.5 %collective-permute-start.4 = (f32[16,8,256]{2,1,0:T(8,128)S(1)}, f32[16,8,256]{2,1,0:T(8,128)S(1)}, u32[]{:S(2)}, u32[]{:S(2)}) collective-permute-start(f32[16,8,256]{2,1,0:T(8,128)S(1)} %get-tuple-element.28.own), channel_id=1, source_target_pairs={{0,16},{4,20},{8,24},{12,28},{16,0},{20,4},{24,8},{28,12},{1,17},{... | collective-permute-start | bytes 393224 | tf_op jit(solution)/shard_map/ppermute | solution.py:553
  13.7 0.4 %collective-permute-start.3 = (f32[16,8,256]{2,1,0:T(8,128)S(1)}, f32[16,8,256]{2,1,0:T(8,128)S(1)}, u32[]{:S(2)}, u32[]{:S(2)}) collective-permute-start(f32[16,8,256]{2,1,0:T(8,128)S(1)} %get-tuple-element.28.own), channel_id=1, source_target_pairs={{0,8},{4,12},{8,0},{12,4},{16,24},{20,28},{24,16},{28,20},{1,9},{5... | collective-permute-start | bytes 393224 | tf_op jit(solution)/shard_map/ppermute | solution.py:553
  14.1 4.7 %explicit.1 = (f32[4,24,8,512]{3,2,1,0:T(8,128)S(1)}, f32[8,8,512]{2,1,0:T(8,128)S(1)}, f32[8,32,512]{2,1,0:T(8,128)S(1)}) custom-call(f32[4,32,8,512]{3,2,1,0:T(8,128)} %fields_ref.5, f32[32,8,512]{2,1,0:T(8,128)S(1)} %copy-done, f32[2,32,8,512]{3,2,1,0:T(8,128)S(1)} %get-tuple-element.23.g0, f32[2,32,8,512]{3,2,1,0:T(8,128)S(1)} %get-tuple-element.24.gn, ...), custom_call_target="tpu_custom_call" | custom-call | flops 5000000000 | tf_op jit(solution)/shard_map/explicit/pallas_call | solution.py:56
  18.8 1.4 %collective-permute-done.4.refs_1_ = f32[16,8,256]{2,1,0:T(8,128)S(1)} collective-permute-done((f32[16,8,256]{2,1,0:T(8,128)S(1)}, f32[16,8,256]{2,1,0:T(8,128)S(1)}, u32[]{:S(2)}, u32[]{:S(2)}) %collective-permute-start.4) | collective-permute-done | bytes 131104 | tf_op jit(solution)/shard_map/ppermute | solution.py:553
  20.2 0.3 collective-permute-done.3.refs_0_
  20.5 0.4 %collective-permute-done.1.high = f32[5,32,512]{2,1,0:T(8,128)S(1)} collective-permute-done((f32[5,32,512]{2,1,0:T(8,128)S(1)}, f32[5,32,512]{2,1,0:T(8,128)S(1)}, u32[]{:S(2)}, u32[]{:S(2)}) %collective-permute-start.1) | collective-permute-done | bytes 327712 | tf_op jit(solution)/shard_map/ppermute | solution.py:573
  20.9 0.3 edge.1
  21.3 0.6 %source.1.t = f32[4,32,8,512]{3,2,1,0:T(8,128)S(1)} custom-call(f32[4,8,8,512]{3,2,1,0:T(8,128)S(1)} %early.1.refs_0_, f32[4,24,8,512]{3,2,1,0:T(8,128)S(1)} %get-tuple-element.33.src, f32[2,32,8,512]{3,2,1,0:T(8,128)S(1)} %get-tuple-element.34.cpr, f32[8,32,512]{2,1,0:T(8,128)S(1)} %get-tuple-element.35.add), custom_call_target="tpu_custom_call" | custom-call | flops 3932160 | bytes 3145728 | tf_op jit(solution)/shard_map/source/pallas_call | solution.py:56
  21.8 0.4 %back.1.refs_2_.part = f32[4,32,8,512]{3,2,1,0:T(8,128)S(1)} custom-call(f32[4,32,8,512]{3,2,1,0:T(8,128)S(1)} %source.1.t, f32[2,32,8,512]{3,2,1,0:T(8,128)S(1)} %get-tuple-element.36.inv, f32[2,32,8,512]{3,2,1,0:T(8,128)S(1)} %get-tuple-element.34.cpr), custom_call_target="tpu_custom_call" | custom-call | flops 2621440 | bytes 3145728 | tf_op jit(solution)/shard_map/back/pallas_call | solution.py:56
  22.2 0.4 %collective-permute-done.6.other = f32[8,8,512]{2,1,0:T(8,128)S(1)} collective-permute-done((f32[8,8,512]{2,1,0:T(8,128)S(1)}, f32[8,8,512]{2,1,0:T(8,128)S(1)}, u32[]{:S(2)}, u32[]{:S(2)}) %collective-permute-start.6) | collective-permute-done | bytes 131104 | tf_op jit(solution)/shard_map/ppermute | solution.py:557
  22.7 2.5 %collective-permute-start.9 = (f32[4,8,256]{2,1,0:T(8,128)S(1)}, f32[4,8,256]{2,1,0:T(8,128)S(1)}, u32[]{:S(2)}, u32[]{:S(2)}) collective-permute-start(f32[4,8,256]{2,1,0:T(8,128)S(1)} %get-tuple-element.38), channel_id=1, source_target_pairs={{0,24},{4,28},{8,16},{12,20},{16,8},{20,12},{24,0},{28,4},{1,25},{... | collective-permute-start | bytes 98312 | tf_op jit(solution)/shard_map/ppermute | solution.py:553
  25.2 0.5 %collective-permute-start.7 = (f32[8,8,256]{2,1,0:T(8,128)S(1)}, f32[8,8,256]{2,1,0:T(8,128)S(1)}, u32[]{:S(2)}, u32[]{:S(2)}) collective-permute-start(f32[8,8,256]{2,1,0:T(8,128)S(1)} %get-tuple-element.37.own), channel_id=1, source_target_pairs={{0,8},{4,12},{8,0},{12,4},{16,24},{20,28},{24,16},{28,20},{1,9},{5... | collective-permute-start | bytes 196616 | tf_op jit(solution)/shard_map/ppermute | solution.py:553
  25.7 0.5 %collective-permute-start.8 = (f32[4,8,256]{2,1,0:T(8,128)S(1)}, f32[4,8,256]{2,1,0:T(8,128)S(1)}, u32[]{:S(2)}, u32[]{:S(2)}) collective-permute-start(f32[4,8,256]{2,1,0:T(8,128)S(1)} %get-tuple-element.38), channel_id=1, source_target_pairs={{0,16},{4,20},{8,24},{12,28},{16,0},{20,4},{24,8},{28,12},{1,17},{... | collective-permute-start | bytes 98312 | tf_op jit(solution)/shard_map/ppermute | solution.py:553
  26.2 1.3 %collective-permute-done.9.refs_0_ = f32[4,8,256]{2,1,0:T(8,128)S(1)} collective-permute-done((f32[4,8,256]{2,1,0:T(8,128)S(1)}, f32[4,8,256]{2,1,0:T(8,128)S(1)}, u32[]{:S(2)}, u32[]{:S(2)}) %collective-permute-start.9) | collective-permute-done | bytes 32800 | tf_op jit(solution)/shard_map/ppermute | solution.py:553
  27.5 2.1 %collective-permute-done.8.refs_1_ = f32[4,8,256]{2,1,0:T(8,128)S(1)} collective-permute-done((f32[4,8,256]{2,1,0:T(8,128)S(1)}, f32[4,8,256]{2,1,0:T(8,128)S(1)}, u32[]{:S(2)}, u32[]{:S(2)}) %collective-permute-start.8) | collective-permute-done | bytes 32800 | tf_op jit(solution)/shard_map/ppermute | solution.py:553
  29.8 1.1 %final_own.1.refs_0_ = f32[4,32,8,512]{3,2,1,0:T(8,128)} custom-call(f32[8,8,256]{2,1,0:T(8,128)S(1)} %settle.1.flux, f32[14,8,512]{2,1,0:T(8,128)S(1)} %get-tuple-element.31.joint, f32[4,8,512]{2,1,0:T(8,128)S(1)} %get-tuple-element.40.diff, f32[4,32,8,512]{3,2,1,0:T(8,128)S(1)} %back.1.refs_2_.part, f32[2,32,8,512]{3,2,1,0:T(8,128)S(1)} %get-tuple-element.23.g0, ...), custom_call_target="tpu_custom_call" | custom-call | flops 1000000000 | tf_op jit(solution)/shard_map/final_own/pallas_call | solution.py:56
  31.0 1.1 %final_other.1 = f32[4,32,8,512]{3,2,1,0:T(8,128)} custom-call(f32[8,8,256]{2,1,0:T(8,128)S(1)} %collective-permute-done.10.flux, f32[14,8,512]{2,1,0:T(8,128)S(1)} %get-tuple-element.31.joint, f32[4,8,512]{2,1,0:T(8,128)S(1)} %get-tuple-element.40.diff, f32[4,32,8,512]{3,2,1,0:T(8,128)S(1)} %back.1.refs_2_.part, ...), custom_call_target="tpu_custom_call", output_to_operand_aliasing={{}: (6, {})} | custom-call | flops 1000000000 | tf_op jit(solution)/shard_map/final_other/pallas_call | solution.py:56
  (15 shorter events, 0.7 us)
Async XLA Ops:
  1.1 6.3 %copy-start = (f32[32,8,512]{2,1,0:T(8,128)S(1)}, f32[32,8,512]{2,1,0:T(8,128)}, u32[]{:S(2)}) copy-start(f32[32,8,512]{2,1,0:T(8,128)} %visc.9) | copy-start | bytes 1572868
  1.1 19.8 %collective-permute-start = (f32[5,32,512]{2,1,0:T(8,128)S(1)}, f32[5,32,512]{2,1,0:T(8,128)S(1)}, u32[]{:S(2)}, u32[]{:S(2)}) collective-permute-start(f32[5,32,512]{2,1,0:T(8,128)S(1)} %cut_last.1.refs_0_.y_last), channel_id=1, source_target_pairs={{0,1},{1,2},{2,3},{3,0},{4,5},{5,6},{6,7},{7,4},{8,9},{9,10},{10,1... | collective-permute-start | bytes 983048 | tf_op jit(solution)/shard_map/ppermute | solution.py:571
  5.2 15.7 %collective-permute-start.1 = (f32[5,32,512]{2,1,0:T(8,128)S(1)}, f32[5,32,512]{2,1,0:T(8,128)S(1)}, u32[]{:S(2)}, u32[]{:S(2)}) collective-permute-start(f32[5,32,512]{2,1,0:T(8,128)S(1)} %cut_first.1.y_first), channel_id=1, source_target_pairs={{1,0},{2,1},{3,2},{0,3},{5,4},{6,5},{7,6},{4,7},{9,8},{10,9},{11,1... | collective-permute-start | bytes 983048 | tf_op jit(solution)/shard_map/ppermute | solution.py:573
  8.3 2.1 %collective-permute-start.2 = (f32[16,8,512]{2,1,0:T(8,128)S(1)}, f32[16,8,512]{2,1,0:T(8,128)S(1)}, u32[]{:S(2)}, u32[]{:S(2)}) collective-permute-start(f32[16,8,512]{2,1,0:T(8,128)S(1)} %get-tuple-element.27.own), channel_id=1, source_target_pairs={{0,4},{4,0},{8,12},{12,8},{16,20},{20,16},{24,28},{28,24},{1,5},{5... | collective-permute-start | bytes 786440 | tf_op jit(solution)/shard_map/ppermute | solution.py:557
  10.5 8.3 %collective-permute-start.5 = (f32[16,8,256]{2,1,0:T(8,128)S(1)}, f32[16,8,256]{2,1,0:T(8,128)S(1)}, u32[]{:S(2)}, u32[]{:S(2)}) collective-permute-start(f32[16,8,256]{2,1,0:T(8,128)S(1)} %get-tuple-element.28.own), channel_id=1, source_target_pairs={{0,24},{4,28},{8,16},{12,20},{16,8},{20,12},{24,0},{28,4},{1,25},{... | collective-permute-start | bytes 393224 | tf_op jit(solution)/shard_map/ppermute | solution.py:553
  13.2 7.0 %collective-permute-start.4 = (f32[16,8,256]{2,1,0:T(8,128)S(1)}, f32[16,8,256]{2,1,0:T(8,128)S(1)}, u32[]{:S(2)}, u32[]{:S(2)}) collective-permute-start(f32[16,8,256]{2,1,0:T(8,128)S(1)} %get-tuple-element.28.own), channel_id=1, source_target_pairs={{0,16},{4,20},{8,24},{12,28},{16,0},{20,4},{24,8},{28,12},{1,17},{... | collective-permute-start | bytes 393224 | tf_op jit(solution)/shard_map/ppermute | solution.py:553
  13.7 6.7 %collective-permute-start.3 = (f32[16,8,256]{2,1,0:T(8,128)S(1)}, f32[16,8,256]{2,1,0:T(8,128)S(1)}, u32[]{:S(2)}, u32[]{:S(2)}) collective-permute-start(f32[16,8,256]{2,1,0:T(8,128)S(1)} %get-tuple-element.28.own), channel_id=1, source_target_pairs={{0,8},{4,12},{8,0},{12,4},{16,24},{20,28},{24,16},{28,20},{1,9},{5... | collective-permute-start | bytes 393224 | tf_op jit(solution)/shard_map/ppermute | solution.py:553
  21.2 1.4 %collective-permute-start.6 = (f32[8,8,512]{2,1,0:T(8,128)S(1)}, f32[8,8,512]{2,1,0:T(8,128)S(1)}, u32[]{:S(2)}, u32[]{:S(2)}) collective-permute-start(f32[8,8,512]{2,1,0:T(8,128)S(1)} %get-tuple-element.30.own), channel_id=1, source_target_pairs={{0,4},{4,0},{8,12},{12,8},{16,20},{20,16},{24,28},{28,24},{1,5},{5... | collective-permute-start | bytes 393224 | tf_op jit(solution)/shard_map/ppermute | solution.py:557
  22.7 4.9 %collective-permute-start.9 = (f32[4,8,256]{2,1,0:T(8,128)S(1)}, f32[4,8,256]{2,1,0:T(8,128)S(1)}, u32[]{:S(2)}, u32[]{:S(2)}) collective-permute-start(f32[4,8,256]{2,1,0:T(8,128)S(1)} %get-tuple-element.38), channel_id=1, source_target_pairs={{0,24},{4,28},{8,16},{12,20},{16,8},{20,12},{24,0},{28,4},{1,25},{... | collective-permute-start | bytes 98312 | tf_op jit(solution)/shard_map/ppermute | solution.py:553
  25.2 4.5 %collective-permute-start.7 = (f32[8,8,256]{2,1,0:T(8,128)S(1)}, f32[8,8,256]{2,1,0:T(8,128)S(1)}, u32[]{:S(2)}, u32[]{:S(2)}) collective-permute-start(f32[8,8,256]{2,1,0:T(8,128)S(1)} %get-tuple-element.37.own), channel_id=1, source_target_pairs={{0,8},{4,12},{8,0},{12,4},{16,24},{20,28},{24,16},{28,20},{1,9},{5... | collective-permute-start | bytes 196616 | tf_op jit(solution)/shard_map/ppermute | solution.py:553
  25.7 3.9 %collective-permute-start.8 = (f32[4,8,256]{2,1,0:T(8,128)S(1)}, f32[4,8,256]{2,1,0:T(8,128)S(1)}, u32[]{:S(2)}, u32[]{:S(2)}) collective-permute-start(f32[4,8,256]{2,1,0:T(8,128)S(1)} %get-tuple-element.38), channel_id=1, source_target_pairs={{0,16},{4,20},{8,24},{12,28},{16,0},{20,4},{24,8},{28,12},{1,17},{... | collective-permute-start | bytes 98312 | tf_op jit(solution)/shard_map/ppermute | solution.py:553
  29.7 1.3 %collective-permute-start.10 = (f32[8,8,256]{2,1,0:T(8,128)S(1)}, f32[8,8,256]{2,1,0:T(8,128)S(1)}, u32[]{:S(2)}, u32[]{:S(2)}) collective-permute-start(f32[8,8,256]{2,1,0:T(8,128)S(1)} %settle.1.flux), channel_id=1, source_target_pairs={{0,4},{4,0},{8,12},{12,8},{16,20},{20,16},{24,28},{28,24},{1,5},{5... | collective-permute-start | bytes 196616 | tf_op jit(solution)/shard_map/ppermute | solution.py:557
where the time goes:
time: 32.4 us; the launch traced here: 32.1 us
  Pallas kernels  13.5 us (42%)
  starting transfers between devices  12.5 us (39%)
  waiting for transfers between devices  5.93 us (18%)
    pallas_call x15, Pallas kernels, call(): pl.pallas_call(kernel, out_shape=out_shape, in_specs=in_specs, out_specs=...  13.5 us
    ppermute x6, starting transfers between devices, gather(): found[d] = lax.ppermute(x, 'line', [(i, i ^ d << 1) for i in range(lines)])  7.11 us
    ppermute x6, waiting for transfers between devices, gather(): found[d] = lax.ppermute(x, 'line', [(i, i ^ d << 1) for i in range(lines)])  5.02 us
    ppermute x1, starting transfers between devices, local(): low = lax.ppermute(y_last, 'col', ring)  3.08 us
    ppermute x1, starting transfers between devices, local(): high = lax.ppermute(y_first, 'col', back_ring)  2.14 us
  transfers between devices with their start and end apart: 11, of which 7 were waited for; matrix products, arithmetic and copies ran while one was open for 0% of the time, Pallas kernels for 34%

commit v1 on v0

--- a/solution.py
+++ b/solution.py
@@ -74,10 +74,12 @@
     return tile
 
 
-def cut_kernel(at, fields, visc, *refs):
-    out, sems = refs[-2:]
-    copies = [pltpu.make_async_copy(fields.at[k, :, at], out.at[k], sems.at[k]) for k in range(4)]
-    copies.append(pltpu.make_async_copy(visc.at[:, at], out.at[4], sems.at[4]))
+def cut_kernel(ny, fields, visc, y_first, y_last, sems):
+    copies = []
+    for j, (at, out) in enumerate(((0, y_first), (ny - 1, y_last))):
+        for k in range(4):
+            copies.append(pltpu.make_async_copy(fields.at[k, :, at], out.at[k], sems.at[j, k]))
+        copies.append(pltpu.make_async_copy(visc.at[:, at], out.at[4], sems.at[j, 4]))
     for copy in copies:
         copy.start()
     for copy in copies:
@@ -507,29 +509,32 @@
     low_side = side_bit(0)
     core = jnp.bitwise_and(lax.axis_index("line"), 1)
     offset = (core if mine else 1 - core) * half
-    copies = []
+    chunks, into = [], []
     for c in range(half // 128):
         near = pl.ds(c * 128, 128)
         z = pl.ds(pl.multiple_of(offset + c * 128, 128), 128)
         across = {plane: joint[plane, :, z] for plane in range(JOINT)}
-        into = [
-            joint_flow(across, k, diff[k, :, z], flux[k, :, near], flux[4 + k, :, near], low_side)
-            for k in range(4)
-        ]
-        for r in range(parts):
-            x = pl.ds(r * (rows // parts), rows // parts)
-            for i in range(x.start, x.start + x.size):
+        chunks.append((near, z))
+        into.append(
+            [
+                joint_flow(across, k, diff[k, :, z], flux[k, :, near], flux[4 + k, :, near], low_side)
+                for k in range(4)
+            ]
+        )
+    copies = []
+    step = rows // parts
+    for r in range(parts):
+        for (near, z), ends in zip(chunks, into):
+            for i in range(r * step, (r + 1) * step):
                 a = [g0[s, i, :, z] for s in range(2)]
                 b = [gn[s, i, :, z] for s in range(2)]
                 for k in range(4):
                     s = KIND[k]
-                    buf[k, i, :, near] = part[k, i, :, z] + (a[s] * into[k][0] + b[s] * into[k][1])
-            copies.append(
-                pltpu.make_async_copy(
-                    buf.at[:, x, :, near], out.at[:, x, :, z], sems.at[c * parts + r]
-                )
-            )
-            copies[-1].start()
+                    buf[k, i, :, near] = part[k, i, :, z] + (a[s] * ends[k][0] + b[s] * ends[k][1])
+        x = pl.ds(r * step, step)
+        lanes = pl.ds(pl.multiple_of(offset, 128), half)
+        copies.append(pltpu.make_async_copy(buf.at[:, x], out.at[:, x, :, lanes], sems.at[r]))
+        copies[-1].start()
     for copy in copies:
         copy.wait()
 
@@ -556,20 +561,16 @@
     def swap(x, level):
         return lax.ppermute(x, "line", [(i, i ^ (1 << level)) for i in range(lines)])
 
-    def cut(at, name, order, flops):
-        return call(
-            functools.partial(cut_kernel, at),
-            name,
-            [(5, rows, nz)],
-            [fields, viscosity] + order,
-            scratch=[pltpu.SemaphoreType.DMA((5,))],
-            in_hbm=(0, 1),
-            flops=flops,
-        )[0]
-
-    y_last = cut(ny - 1, "cut_last", [], 5 * 10**8)
+    y_first, y_last = call(
+        functools.partial(cut_kernel, ny),
+        "cut",
+        [(5, rows, nz), (5, rows, nz)],
+        [fields, viscosity],
+        scratch=[pltpu.SemaphoreType.DMA((2, 5))],
+        in_hbm=(0, 1),
+        moved=2 * cells,
+    )
     low = lax.ppermute(y_last, "col", ring)
-    y_first = cut(0, "cut_first", [y_last], 5 * 10**8)
     high = lax.ppermute(y_first, "col", back_ring)
 
     inv, cpr, g0, gn, w = call(
@@ -666,8 +667,8 @@
         moved=4 * ny * half * 100,
     )
     rest = [pair, diff, part, g0, gn]
-    parts = 4 if rows % 4 == 0 else 1
-    scratch = [VMEM((4, rows, ny, half), F32), pltpu.SemaphoreType.DMA((half // 128 * parts,))]
+    parts = 8 if rows % 8 == 0 else 1
+    scratch = [VMEM((4, rows, ny, half), F32), pltpu.SemaphoreType.DMA((parts,))]
     (out,) = call(
         functools.partial(final_kernel, True, parts),
         "final_own",

time: 32.4 us -> 32 us (0.988)
  Pallas kernels: 13.5 us -> 12.7 us
  waiting for transfers between devices: 5.93 us -> 6.46 us
    pallas_call x15 -> x14, Pallas kernels: 13.5 us -> 12.7 us  [call(): pl.pallas_call(kernel, out_shape=out_shape, in_specs=in_specs, out_specs=...]
    ppermute x1, waiting for transfers between devices: 0.36 us -> 0.91 us  [local(): high = lax.ppermute(y_first, 'col', back_ring)]
  transfers between devices with their start and end apart: 11 -> 11, of which waited for: 7 -> 7; matrix products, arithmetic and copies ran while one was open for 0% -> 0% of each run, Pallas kernels for 34% -> 31%
where the time goes in v1:
time: 32 us; the launch traced here: 31.8 us
  Pallas kernels  12.7 us (40%)
  starting transfers between devices  12.5 us (39%)
  waiting for transfers between devices  6.46 us (20%)
    pallas_call x14, Pallas kernels, call(): pl.pallas_call(kernel, out_shape=out_shape, in_specs=in_specs, out_specs=...  12.7 us
    ppermute x6, starting transfers between devices, gather(): found[d] = lax.ppermute(x, 'line', [(i, i ^ d << 1) for i in range(lines)])  7.11 us
    ppermute x6, waiting for transfers between devices, gather(): found[d] = lax.ppermute(x, 'line', [(i, i ^ d << 1) for i in range(lines)])  5.02 us
    ppermute x1, starting transfers between devices, local(): low = lax.ppermute(y_last, 'col', ring)  3.08 us
    ppermute x1, starting transfers between devices, local(): high = lax.ppermute(y_first, 'col', back_ring)  2.09 us
    ppermute x1, waiting for transfers between devices, local(): high = lax.ppermute(y_first, 'col', back_ring)  0.91 us
  transfers between devices with their start and end apart: 11, of which 7 were waited for; matrix products, arithmetic and copies ran while one was open for 0% of the time, Pallas kernels for 31%

profile of v1, /device:TPU:0, one launch (start us, length us, event | category | flops | bytes accessed | tf_op | source)
XLA Modules:
  0.0 31.8 jit_solution(5927843211141800062)
XLA Ops:
  0.0 1.3 %cut.1 = (f32[5,32,512]{2,1,0:T(8,128)S(1)}, f32[5,32,512]{2,1,0:T(8,128)S(1)}) custom-call(f32[4,32,8,512]{3,2,1,0:T(8,128)} %fields_ref.5, f32[32,8,512]{2,1,0:T(8,128)} %visc.7), custom_call_target="tpu_custom_call" | custom-call | bytes 262144 | tf_op jit(solution)/shard_map/cut/pallas_call | solution.py:56
  1.4 3.1 %collective-permute-start = (f32[5,32,512]{2,1,0:T(8,128)S(1)}, f32[5,32,512]{2,1,0:T(8,128)S(1)}, u32[]{:S(2)}, u32[]{:S(2)}) collective-permute-start(f32[5,32,512]{2,1,0:T(8,128)S(1)} %get-tuple-element.25.y_last), channel_id=1, source_target_pairs={{0,1},{1,2},{2,3},{3,0},{4,5},{5,6},{6,7},{7,4},{8,9},{9,10},{10,1... | collective-permute-start | bytes 983048 | tf_op jit(solution)/shard_map/ppermute | solution.py:573
  4.4 2.1 %collective-permute-start.1 = (f32[5,32,512]{2,1,0:T(8,128)S(1)}, f32[5,32,512]{2,1,0:T(8,128)S(1)}, u32[]{:S(2)}, u32[]{:S(2)}) collective-permute-start(f32[5,32,512]{2,1,0:T(8,128)S(1)} %get-tuple-element.26.y_first), channel_id=1, source_target_pairs={{1,0},{2,1},{3,2},{0,3},{5,4},{6,5},{7,6},{4,7},{9,8},{10,9},{11,1... | collective-permute-start | bytes 983048 | tf_op jit(solution)/shard_map/ppermute | solution.py:574
  6.5 0.9 %factor.1 = (f32[2,32,8,512]{3,2,1,0:T(8,128)S(1)}, f32[2,32,8,512]{3,2,1,0:T(8,128)S(1)}, f32[2,32,8,512]{3,2,1,0:T(8,128)S(1)}, f32[2,32,8,512]{3,2,1,0:T(8,128)S(1)}, f32[16,8,512]{2,1,0:T(8,128)S(1)}) custom-call(f32[4,32,8,512]{3,2,1,0:T(8,128)} %fields_ref.5, f32[32,8,512]{2,1,0:T(8,128)S(1)} %copy-done), custom_call_target="tpu_custom_call" | custom-call | flops 1000000000 | tf_op jit(solution)/shard_map/factor/pallas_call | solution.py:56
  7.6 2.0 %early.1.refs_0_ = f32[4,8,8,512]{3,2,1,0:T(8,128)S(1)} custom-call(f32[4,32,8,512]{3,2,1,0:T(8,128)} %fields_ref.5, f32[32,8,512]{2,1,0:T(8,128)S(1)} %copy-done), custom_call_target="tpu_custom_call" | custom-call | flops 4000000000 | tf_op jit(solution)/shard_map/early/pallas_call | solution.py:56
  9.7 2.7 %collective-permute-start.5 = (f32[16,8,256]{2,1,0:T(8,128)S(1)}, f32[16,8,256]{2,1,0:T(8,128)S(1)}, u32[]{:S(2)}, u32[]{:S(2)}) collective-permute-start(f32[16,8,256]{2,1,0:T(8,128)S(1)} %get-tuple-element.32.own), channel_id=1, source_target_pairs={{0,24},{4,28},{8,16},{12,20},{16,8},{20,12},{24,0},{28,4},{1,25},{... | collective-permute-start | bytes 393224 | tf_op jit(solution)/shard_map/ppermute | solution.py:558
  12.4 0.5 %collective-permute-start.4 = (f32[16,8,256]{2,1,0:T(8,128)S(1)}, f32[16,8,256]{2,1,0:T(8,128)S(1)}, u32[]{:S(2)}, u32[]{:S(2)}) collective-permute-start(f32[16,8,256]{2,1,0:T(8,128)S(1)} %get-tuple-element.32.own), channel_id=1, source_target_pairs={{0,16},{4,20},{8,24},{12,28},{16,0},{20,4},{24,8},{28,12},{1,17},{... | collective-permute-start | bytes 393224 | tf_op jit(solution)/shard_map/ppermute | solution.py:558
  12.9 0.4 %collective-permute-start.3 = (f32[16,8,256]{2,1,0:T(8,128)S(1)}, f32[16,8,256]{2,1,0:T(8,128)S(1)}, u32[]{:S(2)}, u32[]{:S(2)}) collective-permute-start(f32[16,8,256]{2,1,0:T(8,128)S(1)} %get-tuple-element.32.own), channel_id=1, source_target_pairs={{0,8},{4,12},{8,0},{12,4},{16,24},{20,28},{24,16},{28,20},{1,9},{5... | collective-permute-start | bytes 393224 | tf_op jit(solution)/shard_map/ppermute | solution.py:558
  13.2 4.7 %explicit.1 = (f32[4,24,8,512]{3,2,1,0:T(8,128)S(1)}, f32[8,8,512]{2,1,0:T(8,128)S(1)}, f32[8,32,512]{2,1,0:T(8,128)S(1)}) custom-call(f32[4,32,8,512]{3,2,1,0:T(8,128)} %fields_ref.5, f32[32,8,512]{2,1,0:T(8,128)S(1)} %copy-done, f32[2,32,8,512]{3,2,1,0:T(8,128)S(1)} %get-tuple-element.27.g0, f32[2,32,8,512]{3,2,1,0:T(8,128)S(1)} %get-tuple-element.28.gn, ...), custom_call_target="tpu_custom_call" | custom-call | flops 5000000000 | tf_op jit(solution)/shard_map/explicit/pallas_call | solution.py:56
  18.0 1.4 %collective-permute-done.4.refs_1_ = f32[16,8,256]{2,1,0:T(8,128)S(1)} collective-permute-done((f32[16,8,256]{2,1,0:T(8,128)S(1)}, f32[16,8,256]{2,1,0:T(8,128)S(1)}, u32[]{:S(2)}, u32[]{:S(2)}) %collective-permute-start.4) | collective-permute-done | bytes 131104 | tf_op jit(solution)/shard_map/ppermute | solution.py:558
  19.4 0.3 collective-permute-done.3.refs_0_
  19.7 0.9 %collective-permute-done.1.high = f32[5,32,512]{2,1,0:T(8,128)S(1)} collective-permute-done((f32[5,32,512]{2,1,0:T(8,128)S(1)}, f32[5,32,512]{2,1,0:T(8,128)S(1)}, u32[]{:S(2)}, u32[]{:S(2)}) %collective-permute-start.1) | collective-permute-done | bytes 327712 | tf_op jit(solution)/shard_map/ppermute | solution.py:574
  20.6 0.3 edge.1
  21.0 0.6 %source.1.t = f32[4,32,8,512]{3,2,1,0:T(8,128)S(1)} custom-call(f32[4,8,8,512]{3,2,1,0:T(8,128)S(1)} %early.1.refs_0_, f32[4,24,8,512]{3,2,1,0:T(8,128)S(1)} %get-tuple-element.37.src, f32[2,32,8,512]{3,2,1,0:T(8,128)S(1)} %get-tuple-element.38.cpr, f32[8,32,512]{2,1,0:T(8,128)S(1)} %get-tuple-element.39.add), custom_call_target="tpu_custom_call" | custom-call | flops 3932160 | bytes 3145728 | tf_op jit(solution)/shard_map/source/pallas_call | solution.py:56
  21.6 0.4 %back.1.refs_2_.part = f32[4,32,8,512]{3,2,1,0:T(8,128)S(1)} custom-call(f32[4,32,8,512]{3,2,1,0:T(8,128)S(1)} %source.1.t, f32[2,32,8,512]{3,2,1,0:T(8,128)S(1)} %get-tuple-element.40.inv, f32[2,32,8,512]{3,2,1,0:T(8,128)S(1)} %get-tuple-element.38.cpr), custom_call_target="tpu_custom_call" | custom-call | flops 2621440 | bytes 3145728 | tf_op jit(solution)/shard_map/back/pallas_call | solution.py:56
  21.9 0.4 %collective-permute-done.6.other = f32[8,8,512]{2,1,0:T(8,128)S(1)} collective-permute-done((f32[8,8,512]{2,1,0:T(8,128)S(1)}, f32[8,8,512]{2,1,0:T(8,128)S(1)}, u32[]{:S(2)}, u32[]{:S(2)}) %collective-permute-start.6) | collective-permute-done | bytes 131104 | tf_op jit(solution)/shard_map/ppermute | solution.py:562
  22.4 2.5 %collective-permute-start.9 = (f32[4,8,256]{2,1,0:T(8,128)S(1)}, f32[4,8,256]{2,1,0:T(8,128)S(1)}, u32[]{:S(2)}, u32[]{:S(2)}) collective-permute-start(f32[4,8,256]{2,1,0:T(8,128)S(1)} %get-tuple-element.42), channel_id=1, source_target_pairs={{0,24},{4,28},{8,16},{12,20},{16,8},{20,12},{24,0},{28,4},{1,25},{... | collective-permute-start | bytes 98312 | tf_op jit(solution)/shard_map/ppermute | solution.py:558
  24.9 0.5 %collective-permute-start.7 = (f32[8,8,256]{2,1,0:T(8,128)S(1)}, f32[8,8,256]{2,1,0:T(8,128)S(1)}, u32[]{:S(2)}, u32[]{:S(2)}) collective-permute-start(f32[8,8,256]{2,1,0:T(8,128)S(1)} %get-tuple-element.41.own), channel_id=1, source_target_pairs={{0,8},{4,12},{8,0},{12,4},{16,24},{20,28},{24,16},{28,20},{1,9},{5... | collective-permute-start | bytes 196616 | tf_op jit(solution)/shard_map/ppermute | solution.py:558
  25.4 0.5 %collective-permute-start.8 = (f32[4,8,256]{2,1,0:T(8,128)S(1)}, f32[4,8,256]{2,1,0:T(8,128)S(1)}, u32[]{:S(2)}, u32[]{:S(2)}) collective-permute-start(f32[4,8,256]{2,1,0:T(8,128)S(1)} %get-tuple-element.42), channel_id=1, source_target_pairs={{0,16},{4,20},{8,24},{12,28},{16,0},{20,4},{24,8},{28,12},{1,17},{... | collective-permute-start | bytes 98312 | tf_op jit(solution)/shard_map/ppermute | solution.py:558
  25.9 1.3 %collective-permute-done.9.refs_0_ = f32[4,8,256]{2,1,0:T(8,128)S(1)} collective-permute-done((f32[4,8,256]{2,1,0:T(8,128)S(1)}, f32[4,8,256]{2,1,0:T(8,128)S(1)}, u32[]{:S(2)}, u32[]{:S(2)}) %collective-permute-start.9) | collective-permute-done | bytes 32800 | tf_op jit(solution)/shard_map/ppermute | solution.py:558
  27.3 2.1 %collective-permute-done.8.refs_1_ = f32[4,8,256]{2,1,0:T(8,128)S(1)} collective-permute-done((f32[4,8,256]{2,1,0:T(8,128)S(1)}, f32[4,8,256]{2,1,0:T(8,128)S(1)}, u32[]{:S(2)}, u32[]{:S(2)}) %collective-permute-start.8) | collective-permute-done | bytes 32800 | tf_op jit(solution)/shard_map/ppermute | solution.py:558
  29.5 1.1 %final_own.1.refs_0_ = f32[4,32,8,512]{3,2,1,0:T(8,128)} custom-call(f32[8,8,256]{2,1,0:T(8,128)S(1)} %settle.1.flux, f32[14,8,512]{2,1,0:T(8,128)S(1)} %get-tuple-element.35.joint, f32[4,8,512]{2,1,0:T(8,128)S(1)} %get-tuple-element.44.diff, f32[4,32,8,512]{3,2,1,0:T(8,128)S(1)} %back.1.refs_2_.part, f32[2,32,8,512]{3,2,1,0:T(8,128)S(1)} %get-tuple-element.27.g0, ...), custom_call_target="tpu_custom_call" | custom-call | flops 1000000000 | tf_op jit(solution)/shard_map/final_own/pallas_call | solution.py:56
  30.6 0.1 collective-permute-done.10.flux
  30.7 1.1 %final_other.1 = f32[4,32,8,512]{3,2,1,0:T(8,128)} custom-call(f32[8,8,256]{2,1,0:T(8,128)S(1)} %collective-permute-done.10.flux, f32[14,8,512]{2,1,0:T(8,128)S(1)} %get-tuple-element.35.joint, f32[4,8,512]{2,1,0:T(8,128)S(1)} %get-tuple-element.44.diff, f32[4,32,8,512]{3,2,1,0:T(8,128)S(1)} %back.1.refs_2_.part, ...), custom_call_target="tpu_custom_call", output_to_operand_aliasing={{}: (6, {})} | custom-call | flops 1000000000 | tf_op jit(solution)/shard_map/final_other/pallas_call | solution.py:56
  (14 shorter events, 0.5 us)
Async XLA Ops:
  0.0 6.5 %copy-start = (f32[32,8,512]{2,1,0:T(8,128)S(1)}, f32[32,8,512]{2,1,0:T(8,128)}, u32[]{:S(2)}) copy-start(f32[32,8,512]{2,1,0:T(8,128)} %visc.7) | copy-start | bytes 1572868
  1.4 18.4 %collective-permute-start = (f32[5,32,512]{2,1,0:T(8,128)S(1)}, f32[5,32,512]{2,1,0:T(8,128)S(1)}, u32[]{:S(2)}, u32[]{:S(2)}) collective-permute-start(f32[5,32,512]{2,1,0:T(8,128)S(1)} %get-tuple-element.25.y_last), channel_id=1, source_target_pairs={{0,1},{1,2},{2,3},{3,0},{4,5},{5,6},{6,7},{7,4},{8,9},{9,10},{10,1... | collective-permute-start | bytes 983048 | tf_op jit(solution)/shard_map/ppermute | solution.py:573
  4.4 16.2 %collective-permute-start.1 = (f32[5,32,512]{2,1,0:T(8,128)S(1)}, f32[5,32,512]{2,1,0:T(8,128)S(1)}, u32[]{:S(2)}, u32[]{:S(2)}) collective-permute-start(f32[5,32,512]{2,1,0:T(8,128)S(1)} %get-tuple-element.26.y_first), channel_id=1, source_target_pairs={{1,0},{2,1},{3,2},{0,3},{5,4},{6,5},{7,6},{4,7},{9,8},{10,9},{11,1... | collective-permute-start | bytes 983048 | tf_op jit(solution)/shard_map/ppermute | solution.py:574
  7.5 2.1 %collective-permute-start.2 = (f32[16,8,512]{2,1,0:T(8,128)S(1)}, f32[16,8,512]{2,1,0:T(8,128)S(1)}, u32[]{:S(2)}, u32[]{:S(2)}) collective-permute-start(f32[16,8,512]{2,1,0:T(8,128)S(1)} %get-tuple-element.31.own), channel_id=1, source_target_pairs={{0,4},{4,0},{8,12},{12,8},{16,20},{20,16},{24,28},{28,24},{1,5},{5... | collective-permute-start | bytes 786440 | tf_op jit(solution)/shard_map/ppermute | solution.py:562
  9.7 8.3 %collective-permute-start.5 = (f32[16,8,256]{2,1,0:T(8,128)S(1)}, f32[16,8,256]{2,1,0:T(8,128)S(1)}, u32[]{:S(2)}, u32[]{:S(2)}) collective-permute-start(f32[16,8,256]{2,1,0:T(8,128)S(1)} %get-tuple-element.32.own), channel_id=1, source_target_pairs={{0,24},{4,28},{8,16},{12,20},{16,8},{20,12},{24,0},{28,4},{1,25},{... | collective-permute-start | bytes 393224 | tf_op jit(solution)/shard_map/ppermute | solution.py:558
  12.4 7.0 %collective-permute-start.4 = (f32[16,8,256]{2,1,0:T(8,128)S(1)}, f32[16,8,256]{2,1,0:T(8,128)S(1)}, u32[]{:S(2)}, u32[]{:S(2)}) collective-permute-start(f32[16,8,256]{2,1,0:T(8,128)S(1)} %get-tuple-element.32.own), channel_id=1, source_target_pairs={{0,16},{4,20},{8,24},{12,28},{16,0},{20,4},{24,8},{28,12},{1,17},{... | collective-permute-start | bytes 393224 | tf_op jit(solution)/shard_map/ppermute | solution.py:558
  12.9 6.7 %collective-permute-start.3 = (f32[16,8,256]{2,1,0:T(8,128)S(1)}, f32[16,8,256]{2,1,0:T(8,128)S(1)}, u32[]{:S(2)}, u32[]{:S(2)}) collective-permute-start(f32[16,8,256]{2,1,0:T(8,128)S(1)} %get-tuple-element.32.own), channel_id=1, source_target_pairs={{0,8},{4,12},{8,0},{12,4},{16,24},{20,28},{24,16},{28,20},{1,9},{5... | collective-permute-start | bytes 393224 | tf_op jit(solution)/shard_map/ppermute | solution.py:558
  20.9 1.4 %collective-permute-start.6 = (f32[8,8,512]{2,1,0:T(8,128)S(1)}, f32[8,8,512]{2,1,0:T(8,128)S(1)}, u32[]{:S(2)}, u32[]{:S(2)}) collective-permute-start(f32[8,8,512]{2,1,0:T(8,128)S(1)} %get-tuple-element.34.own), channel_id=1, source_target_pairs={{0,4},{4,0},{8,12},{12,8},{16,20},{20,16},{24,28},{28,24},{1,5},{5... | collective-permute-start | bytes 393224 | tf_op jit(solution)/shard_map/ppermute | solution.py:562
  22.4 4.9 %collective-permute-start.9 = (f32[4,8,256]{2,1,0:T(8,128)S(1)}, f32[4,8,256]{2,1,0:T(8,128)S(1)}, u32[]{:S(2)}, u32[]{:S(2)}) collective-permute-start(f32[4,8,256]{2,1,0:T(8,128)S(1)} %get-tuple-element.42), channel_id=1, source_target_pairs={{0,24},{4,28},{8,16},{12,20},{16,8},{20,12},{24,0},{28,4},{1,25},{... | collective-permute-start | bytes 98312 | tf_op jit(solution)/shard_map/ppermute | solution.py:558
  24.9 4.5 %collective-permute-start.7 = (f32[8,8,256]{2,1,0:T(8,128)S(1)}, f32[8,8,256]{2,1,0:T(8,128)S(1)}, u32[]{:S(2)}, u32[]{:S(2)}) collective-permute-start(f32[8,8,256]{2,1,0:T(8,128)S(1)} %get-tuple-element.41.own), channel_id=1, source_target_pairs={{0,8},{4,12},{8,0},{12,4},{16,24},{20,28},{24,16},{28,20},{1,9},{5... | collective-permute-start | bytes 196616 | tf_op jit(solution)/shard_map/ppermute | solution.py:558
  25.4 3.9 %collective-permute-start.8 = (f32[4,8,256]{2,1,0:T(8,128)S(1)}, f32[4,8,256]{2,1,0:T(8,128)S(1)}, u32[]{:S(2)}, u32[]{:S(2)}) collective-permute-start(f32[4,8,256]{2,1,0:T(8,128)S(1)} %get-tuple-element.42), channel_id=1, source_target_pairs={{0,16},{4,20},{8,24},{12,28},{16,0},{20,4},{24,8},{28,12},{1,17},{... | collective-permute-start | bytes 98312 | tf_op jit(solution)/shard_map/ppermute | solution.py:558
  29.4 1.3 %collective-permute-start.10 = (f32[8,8,256]{2,1,0:T(8,128)S(1)}, f32[8,8,256]{2,1,0:T(8,128)S(1)}, u32[]{:S(2)}, u32[]{:S(2)}) collective-permute-start(f32[8,8,256]{2,1,0:T(8,128)S(1)} %settle.1.flux), channel_id=1, source_target_pairs={{0,4},{4,0},{8,12},{12,8},{16,20},{20,16},{24,28},{28,24},{1,5},{5... | collective-permute-start | bytes 196616 | tf_op jit(solution)/shard_map/ppermute | solution.py:562

commit v2 on v1

--- a/solution.py
+++ b/solution.py
@@ -252,8 +252,11 @@
 
 
 def edge_kernel(rows, ny, y_last, y_first, low, high, ends, p, *refs):
-    add, out = refs[-2:]
-    nz = out.shape[2]
+    add, keep, send = refs[-3:]
+    nz = add.shape[2]
+    half = nz // 2
+    low_core = side_bit(0)
+    values = {}
     sub = lax.broadcasted_iota(jnp.int32, (ny, 128), 0)
     rate = 0.5 * ADVECTION
     for j in range(nz // 128):
@@ -280,7 +283,13 @@
             add_low = jnp.sum(sums[0][slot], axis=0, keepdims=True)
             add_high = jnp.sum(sums[1][slot], axis=0, keepdims=True)
             both = jnp.where(sub == 0, add_low, jnp.where(sub == ny - 1, add_high, 0.0))
-            out[slot, :, z] = p[slot, :, z] + both
+            values[slot, j] = p[slot, :, z] + both
+    for slot in range(8):
+        for c in range(half // 128):
+            near = pl.ds(c * 128, 128)
+            one, two = values[slot, c], values[slot, c + half // 128]
+            keep[slot, :, near] = jnp.where(low_core, one, two)
+            send[slot, :, near] = jnp.where(low_core, two, one)
 
 
 def side_bit(level):
@@ -327,9 +336,9 @@
     low_side = side_bit(0)
     planes = range(PLANES)
     found, new = join(*sided(low_side, {p: own[p] for p in planes}, {p: other[p] for p in planes}))
+    width = out.shape[2]
     for plane in range(JOINT):
-        joint[plane] = found[plane]
-    width = out.shape[2]
+        joint[plane] = jnp.where(low_side, found[plane][:, :width], found[plane][:, width:])
     for plane in planes:
         out[plane] = jnp.where(low_side, new[plane][:, :width], new[plane][:, width:])
 
@@ -430,13 +439,10 @@
     out, diff = refs[levels : levels + 2]
     shares = refs[levels + 2 :]
     low_side = side_bit(0)
-    width = out.shape[2]
     left, right = sided(low_side, {p: own[p] for p in range(8)}, {p: other[p] for p in range(8)})
     ends = {}
     for k in range(4):
-        diff[k], first, last = up(joint, k, left, right)
-        ends[k] = jnp.where(low_side, first[:, :width], first[:, width:])
-        ends[4 + k] = jnp.where(low_side, last[:, :width], last[:, width:])
+        diff[k], ends[k], ends[4 + k] = up(joint, k, left, right)
         out[k] = ends[k]
         out[4 + k] = ends[4 + k]
     for level in range(1, levels - 1):
@@ -474,7 +480,8 @@
 
 def settle_kernel(levels, own, *refs):
     near, refs = refs[: levels - 1], refs[levels - 1 :]
-    far, joints, out = refs[: levels - 2], refs[levels - 2 : -1], refs[-1]
+    far, joints = refs[: levels - 2], refs[levels - 2 : 2 * levels - 3]
+    pair, diff, out, send = refs[2 * levels - 3 :]
     ends = {p: own[p] for p in range(8)}
     diffs = []
     for level in range(1, levels):
@@ -499,42 +506,41 @@
             first, last = joint_flow(
                 joints[level - 1].at[0], k, diffs[level - 1][k], first, last, side_bit(level)
             )
-        out[k] = first
-        out[4 + k] = last
-
-
-def final_kernel(mine, parts, flux, joint, diff, part, g0, gn, *refs):
+        low_side = side_bit(0)
+        s = KIND[k]
+        flow = pair[R_ + s] * (diff[k] + pair[GA + s] * first - pair[GB + s] * last)
+        low_last, high_first = pair[CA + k] - flow, pair[CB + k] + flow
+        out[k] = jnp.where(low_side, first, high_first)
+        out[4 + k] = jnp.where(low_side, low_last, last)
+        send[k] = jnp.where(low_side, high_first, first)
+        send[4 + k] = jnp.where(low_side, last, low_last)
+
+
+def final_kernel(mine, parts, flux, part, g0, gn, *refs):
     out, buf, sems = refs[-3:]
     rows, half = buf.shape[1], buf.shape[3]
-    low_side = side_bit(0)
     core = jnp.bitwise_and(lax.axis_index("line"), 1)
     offset = (core if mine else 1 - core) * half
-    chunks, into = [], []
+    step = rows // parts
+    copies = []
     for c in range(half // 128):
         near = pl.ds(c * 128, 128)
         z = pl.ds(pl.multiple_of(offset + c * 128, 128), 128)
-        across = {plane: joint[plane, :, z] for plane in range(JOINT)}
-        chunks.append((near, z))
-        into.append(
-            [
-                joint_flow(across, k, diff[k, :, z], flux[k, :, near], flux[4 + k, :, near], low_side)
-                for k in range(4)
-            ]
-        )
-    copies = []
-    step = rows // parts
-    for r in range(parts):
-        for (near, z), ends in zip(chunks, into):
+        into = [flux[k, :, near] for k in range(8)]
+        for r in range(parts):
             for i in range(r * step, (r + 1) * step):
                 a = [g0[s, i, :, z] for s in range(2)]
                 b = [gn[s, i, :, z] for s in range(2)]
                 for k in range(4):
                     s = KIND[k]
-                    buf[k, i, :, near] = part[k, i, :, z] + (a[s] * ends[k][0] + b[s] * ends[k][1])
-        x = pl.ds(r * step, step)
-        lanes = pl.ds(pl.multiple_of(offset, 128), half)
-        copies.append(pltpu.make_async_copy(buf.at[:, x], out.at[:, x, :, lanes], sems.at[r]))
-        copies[-1].start()
+                    buf[k, i, :, near] = part[k, i, :, z] + (a[s] * into[k] + b[s] * into[4 + k])
+            x = pl.ds(r * step, step)
+            copies.append(
+                pltpu.make_async_copy(
+                    buf.at[:, x, :, near], out.at[:, x, :, z], sems.at[c * parts + r]
+                )
+            )
+            copies[-1].start()
     for copy in copies:
         copy.wait()
 
@@ -604,7 +610,7 @@
     pair, w = call(
         pair_kernel,
         "pair",
-        [(JOINT, ny, nz), (PLANES, ny, half)],
+        [(JOINT, ny, half), (PLANES, ny, half)],
         [w, swap(w, 0), early],
         moved=4 * ny * nz * 60,
     )
@@ -620,10 +626,10 @@
     )
     joints, consts = list(found[: levels - 1]), list(found[levels - 1 :])
 
-    add, p = call(
+    add, p, sent = call(
         functools.partial(edge_kernel, rows, ny),
         "edge",
-        [(8, rows, nz), (8, ny, nz)],
+        [(8, rows, nz), (8, ny, half), (8, ny, half)],
         [y_last, y_first, low, high, ends, p, joints[0]],
         flops=5 * 10**8,
     )
@@ -646,8 +652,8 @@
     p, diff, *shares = call(
         functools.partial(up_kernel, levels),
         "up",
-        [(8, ny, half), (4, ny, nz)] + [(width, ny, half) for width in widths],
-        [p, swap(p, 0), pair] + joints + [part],
+        [(8, ny, half), (4, ny, half)] + [(width, ny, half) for width in widths],
+        [p, swap(sent, 0), pair] + joints + [part],
         moved=4 * ny * nz * 40,
     )
     others = dict(enumerate(gather([None, p] + shares), 1))
@@ -659,16 +665,16 @@
         list(others.values()) + consts,
         flops=6 * 10**8,
     )
-    (flux,) = call(
+    flux, sent = call(
         functools.partial(settle_kernel, levels),
         "settle",
-        [(8, ny, half)],
-        [p] + near + list(beside) + joints,
+        [(8, ny, half)] * 2,
+        [p] + near + list(beside) + joints + [pair, diff],
         moved=4 * ny * half * 100,
     )
-    rest = [pair, diff, part, g0, gn]
-    parts = 8 if rows % 8 == 0 else 1
-    scratch = [VMEM((4, rows, ny, half), F32), pltpu.SemaphoreType.DMA((parts,))]
+    rest = [part, g0, gn]
+    parts = 4 if rows % 4 == 0 else 1
+    scratch = [VMEM((4, rows, ny, half), F32), pltpu.SemaphoreType.DMA((half // 128 * parts,))]
     (out,) = call(
         functools.partial(final_kernel, True, parts),
         "final_own",
@@ -682,11 +688,11 @@
         functools.partial(final_kernel, False, parts),
         "final_other",
         [(4,) + block],
-        [swap(flux, 0)] + rest + [out],
+        [swap(sent, 0)] + rest + [out],
         scratch=scratch,
-        in_hbm=(6,),
+        in_hbm=(4,),
         out_hbm=(0,),
-        aliases={6: 0},
+        aliases={4: 0},
         flops=10**9,
     )
     return out

time: 32 us -> 31.9 us (level)
  no operation moved by 1% of the time
where the time goes in v2:
time: 31.9 us; the launch traced here: 31.7 us
  Pallas kernels  12.7 us (40%)
  starting transfers between devices  12.5 us (39%)
  waiting for transfers between devices  6.38 us (20%)
    pallas_call x14, Pallas kernels, call(): pl.pallas_call(kernel, out_shape=out_shape, in_specs=in_specs, out_specs=...  12.7 us
    ppermute x6, starting transfers between devices, gather(): found[d] = lax.ppermute(x, 'line', [(i, i ^ d << 1) for i in range(lines)])  7.11 us
    ppermute x6, waiting for transfers between devices, gather(): found[d] = lax.ppermute(x, 'line', [(i, i ^ d << 1) for i in range(lines)])  5.02 us
    ppermute x1, starting transfers between devices, local(): low = lax.ppermute(y_last, 'col', ring)  3.08 us
    ppermute x1, starting transfers between devices, local(): high = lax.ppermute(y_first, 'col', back_ring)  2.09 us
    ppermute x1, waiting for transfers between devices, local(): high = lax.ppermute(y_first, 'col', back_ring)  0.9 us
  transfers between devices with their start and end apart: 11, of which 7 were waited for; matrix products, arithmetic and copies ran while one was open for 0% of the time, Pallas kernels for 31%

profile of v2, /device:TPU:0, one launch (start us, length us, event | category | flops | bytes accessed | tf_op | source)
XLA Modules:
  0.0 31.7 jit_solution(7255586299325768984)
XLA Ops:
  0.0 1.3 %cut.1 = (f32[5,32,512]{2,1,0:T(8,128)S(1)}, f32[5,32,512]{2,1,0:T(8,128)S(1)}) custom-call(f32[4,32,8,512]{3,2,1,0:T(8,128)} %fields_ref.5, f32[32,8,512]{2,1,0:T(8,128)} %visc.7), custom_call_target="tpu_custom_call" | custom-call | bytes 262144 | tf_op jit(solution)/shard_map/cut/pallas_call | solution.py:56
  1.4 3.1 %collective-permute-start = (f32[5,32,512]{2,1,0:T(8,128)S(1)}, f32[5,32,512]{2,1,0:T(8,128)S(1)}, u32[]{:S(2)}, u32[]{:S(2)}) collective-permute-start(f32[5,32,512]{2,1,0:T(8,128)S(1)} %get-tuple-element.28.y_last), channel_id=1, source_target_pairs={{0,1},{1,2},{2,3},{3,0},{4,5},{5,6},{6,7},{7,4},{8,9},{9,10},{10,1... | collective-permute-start | bytes 983048 | tf_op jit(solution)/shard_map/ppermute | solution.py:579
  4.4 2.1 %collective-permute-start.1 = (f32[5,32,512]{2,1,0:T(8,128)S(1)}, f32[5,32,512]{2,1,0:T(8,128)S(1)}, u32[]{:S(2)}, u32[]{:S(2)}) collective-permute-start(f32[5,32,512]{2,1,0:T(8,128)S(1)} %get-tuple-element.29.y_first), channel_id=1, source_target_pairs={{1,0},{2,1},{3,2},{0,3},{5,4},{6,5},{7,6},{4,7},{9,8},{10,9},{11,1... | collective-permute-start | bytes 983048 | tf_op jit(solution)/shard_map/ppermute | solution.py:580
  6.5 0.9 %factor.1 = (f32[2,32,8,512]{3,2,1,0:T(8,128)S(1)}, f32[2,32,8,512]{3,2,1,0:T(8,128)S(1)}, f32[2,32,8,512]{3,2,1,0:T(8,128)S(1)}, f32[2,32,8,512]{3,2,1,0:T(8,128)S(1)}, f32[16,8,512]{2,1,0:T(8,128)S(1)}) custom-call(f32[4,32,8,512]{3,2,1,0:T(8,128)} %fields_ref.5, f32[32,8,512]{2,1,0:T(8,128)S(1)} %copy-done), custom_call_target="tpu_custom_call" | custom-call | flops 1000000000 | tf_op jit(solution)/shard_map/factor/pallas_call | solution.py:56
  7.6 2.0 %early.1.refs_0_ = f32[4,8,8,512]{3,2,1,0:T(8,128)S(1)} custom-call(f32[4,32,8,512]{3,2,1,0:T(8,128)} %fields_ref.5, f32[32,8,512]{2,1,0:T(8,128)S(1)} %copy-done), custom_call_target="tpu_custom_call" | custom-call | flops 4000000000 | tf_op jit(solution)/shard_map/early/pallas_call | solution.py:56
  9.7 2.7 %collective-permute-start.5 = (f32[16,8,256]{2,1,0:T(8,128)S(1)}, f32[16,8,256]{2,1,0:T(8,128)S(1)}, u32[]{:S(2)}, u32[]{:S(2)}) collective-permute-start(f32[16,8,256]{2,1,0:T(8,128)S(1)} %get-tuple-element.35.own), channel_id=1, source_target_pairs={{0,24},{4,28},{8,16},{12,20},{16,8},{20,12},{24,0},{28,4},{1,25},{... | collective-permute-start | bytes 393224 | tf_op jit(solution)/shard_map/ppermute | solution.py:564
  12.4 0.5 %collective-permute-start.4 = (f32[16,8,256]{2,1,0:T(8,128)S(1)}, f32[16,8,256]{2,1,0:T(8,128)S(1)}, u32[]{:S(2)}, u32[]{:S(2)}) collective-permute-start(f32[16,8,256]{2,1,0:T(8,128)S(1)} %get-tuple-element.35.own), channel_id=1, source_target_pairs={{0,16},{4,20},{8,24},{12,28},{16,0},{20,4},{24,8},{28,12},{1,17},{... | collective-permute-start | bytes 393224 | tf_op jit(solution)/shard_map/ppermute | solution.py:564
  12.9 0.4 %collective-permute-start.3 = (f32[16,8,256]{2,1,0:T(8,128)S(1)}, f32[16,8,256]{2,1,0:T(8,128)S(1)}, u32[]{:S(2)}, u32[]{:S(2)}) collective-permute-start(f32[16,8,256]{2,1,0:T(8,128)S(1)} %get-tuple-element.35.own), channel_id=1, source_target_pairs={{0,8},{4,12},{8,0},{12,4},{16,24},{20,28},{24,16},{28,20},{1,9},{5... | collective-permute-start | bytes 393224 | tf_op jit(solution)/shard_map/ppermute | solution.py:564
  13.2 4.7 %explicit.1 = (f32[4,24,8,512]{3,2,1,0:T(8,128)S(1)}, f32[8,8,512]{2,1,0:T(8,128)S(1)}, f32[8,32,512]{2,1,0:T(8,128)S(1)}) custom-call(f32[4,32,8,512]{3,2,1,0:T(8,128)} %fields_ref.5, f32[32,8,512]{2,1,0:T(8,128)S(1)} %copy-done, f32[2,32,8,512]{3,2,1,0:T(8,128)S(1)} %get-tuple-element.30.g0, f32[2,32,8,512]{3,2,1,0:T(8,128)S(1)} %get-tuple-element.31.gn, ...), custom_call_target="tpu_custom_call" | custom-call | flops 5000000000 | tf_op jit(solution)/shard_map/explicit/pallas_call | solution.py:56
  18.0 1.4 %collective-permute-done.4.refs_1_ = f32[16,8,256]{2,1,0:T(8,128)S(1)} collective-permute-done((f32[16,8,256]{2,1,0:T(8,128)S(1)}, f32[16,8,256]{2,1,0:T(8,128)S(1)}, u32[]{:S(2)}, u32[]{:S(2)}) %collective-permute-start.4) | collective-permute-done | bytes 131104 | tf_op jit(solution)/shard_map/ppermute | solution.py:564
  19.4 0.3 collective-permute-done.3.refs_0_
  19.7 0.9 %collective-permute-done.1.high = f32[5,32,512]{2,1,0:T(8,128)S(1)} collective-permute-done((f32[5,32,512]{2,1,0:T(8,128)S(1)}, f32[5,32,512]{2,1,0:T(8,128)S(1)}, u32[]{:S(2)}, u32[]{:S(2)}) %collective-permute-start.1) | collective-permute-done | bytes 327712 | tf_op jit(solution)/shard_map/ppermute | solution.py:580
  20.6 0.3 edge.1
  21.0 0.6 %source.1.t = f32[4,32,8,512]{3,2,1,0:T(8,128)S(1)} custom-call(f32[4,8,8,512]{3,2,1,0:T(8,128)S(1)} %early.1.refs_0_, f32[4,24,8,512]{3,2,1,0:T(8,128)S(1)} %get-tuple-element.41.src, f32[2,32,8,512]{3,2,1,0:T(8,128)S(1)} %get-tuple-element.42.cpr, f32[8,32,512]{2,1,0:T(8,128)S(1)} %get-tuple-element.43.add), custom_call_target="tpu_custom_call" | custom-call | flops 3932160 | bytes 3145728 | tf_op jit(solution)/shard_map/source/pallas_call | solution.py:56
  21.6 0.4 %back.1.refs_2_.part = f32[4,32,8,512]{3,2,1,0:T(8,128)S(1)} custom-call(f32[4,32,8,512]{3,2,1,0:T(8,128)S(1)} %source.1.t, f32[2,32,8,512]{3,2,1,0:T(8,128)S(1)} %get-tuple-element.44.inv, f32[2,32,8,512]{3,2,1,0:T(8,128)S(1)} %get-tuple-element.42.cpr), custom_call_target="tpu_custom_call" | custom-call | flops 2621440 | bytes 3145728 | tf_op jit(solution)/shard_map/back/pallas_call | solution.py:56
  21.9 0.3 collective-permute-done.6.other
  22.3 2.5 %collective-permute-start.9 = (f32[4,8,256]{2,1,0:T(8,128)S(1)}, f32[4,8,256]{2,1,0:T(8,128)S(1)}, u32[]{:S(2)}, u32[]{:S(2)}) collective-permute-start(f32[4,8,256]{2,1,0:T(8,128)S(1)} %get-tuple-element.46), channel_id=1, source_target_pairs={{0,24},{4,28},{8,16},{12,20},{16,8},{20,12},{24,0},{28,4},{1,25},{... | collective-permute-start | bytes 98312 | tf_op jit(solution)/shard_map/ppermute | solution.py:564
  24.8 0.5 %collective-permute-start.7 = (f32[8,8,256]{2,1,0:T(8,128)S(1)}, f32[8,8,256]{2,1,0:T(8,128)S(1)}, u32[]{:S(2)}, u32[]{:S(2)}) collective-permute-start(f32[8,8,256]{2,1,0:T(8,128)S(1)} %get-tuple-element.45.own), channel_id=1, source_target_pairs={{0,8},{4,12},{8,0},{12,4},{16,24},{20,28},{24,16},{28,20},{1,9},{5... | collective-permute-start | bytes 196616 | tf_op jit(solution)/shard_map/ppermute | solution.py:564
  25.3 0.5 %collective-permute-start.8 = (f32[4,8,256]{2,1,0:T(8,128)S(1)}, f32[4,8,256]{2,1,0:T(8,128)S(1)}, u32[]{:S(2)}, u32[]{:S(2)}) collective-permute-start(f32[4,8,256]{2,1,0:T(8,128)S(1)} %get-tuple-element.46), channel_id=1, source_target_pairs={{0,16},{4,20},{8,24},{12,28},{16,0},{20,4},{24,8},{28,12},{1,17},{... | collective-permute-start | bytes 98312 | tf_op jit(solution)/shard_map/ppermute | solution.py:564
  25.8 1.3 %collective-permute-done.9.refs_0_ = f32[4,8,256]{2,1,0:T(8,128)S(1)} collective-permute-done((f32[4,8,256]{2,1,0:T(8,128)S(1)}, f32[4,8,256]{2,1,0:T(8,128)S(1)}, u32[]{:S(2)}, u32[]{:S(2)}) %collective-permute-start.9) | collective-permute-done | bytes 32800 | tf_op jit(solution)/shard_map/ppermute | solution.py:564
  27.2 2.1 %collective-permute-done.8.refs_1_ = f32[4,8,256]{2,1,0:T(8,128)S(1)} collective-permute-done((f32[4,8,256]{2,1,0:T(8,128)S(1)}, f32[4,8,256]{2,1,0:T(8,128)S(1)}, u32[]{:S(2)}, u32[]{:S(2)}) %collective-permute-start.8) | collective-permute-done | bytes 32800 | tf_op jit(solution)/shard_map/ppermute | solution.py:564
  29.4 1.1 %final_own.1.refs_0_ = f32[4,32,8,512]{3,2,1,0:T(8,128)} custom-call(f32[8,8,256]{2,1,0:T(8,128)S(1)} %get-tuple-element.50.flux, f32[4,32,8,512]{3,2,1,0:T(8,128)S(1)} %back.1.refs_2_.part, f32[2,32,8,512]{3,2,1,0:T(8,128)S(1)} %get-tuple-element.30.g0, f32[2,32,8,512]{3,2,1,0:T(8,128)S(1)} %get-tuple-element.31.gn), custom_call_target="tpu_custom_call" | custom-call | flops 1000000000 | tf_op jit(solution)/shard_map/final_own/pallas_call | solution.py:56
  30.5 0.2 collective-permute-done.10.flux
  30.6 1.1 %final_other.1 = f32[4,32,8,512]{3,2,1,0:T(8,128)} custom-call(f32[8,8,256]{2,1,0:T(8,128)S(1)} %collective-permute-done.10.flux, f32[4,32,8,512]{3,2,1,0:T(8,128)S(1)} %back.1.refs_2_.part, f32[2,32,8,512]{3,2,1,0:T(8,128)S(1)} %get-tuple-element.30.g0, f32[2,32,8,512]{3,2,1,0:T(8,128)S(1)} %get-tuple-element.31.gn, ...), custom_call_target="tpu_custom_call", output_to_operand_aliasing={{}: (4, {})} | custom-call | flops 1000000000 | tf_op jit(solution)/shard_map/final_other/pallas_call | solution.py:56
  (14 shorter events, 0.5 us)
Async XLA Ops:
  0.0 6.5 %copy-start = (f32[32,8,512]{2,1,0:T(8,128)S(1)}, f32[32,8,512]{2,1,0:T(8,128)}, u32[]{:S(2)}) copy-start(f32[32,8,512]{2,1,0:T(8,128)} %visc.7) | copy-start | bytes 1572868
  1.4 18.4 %collective-permute-start = (f32[5,32,512]{2,1,0:T(8,128)S(1)}, f32[5,32,512]{2,1,0:T(8,128)S(1)}, u32[]{:S(2)}, u32[]{:S(2)}) collective-permute-start(f32[5,32,512]{2,1,0:T(8,128)S(1)} %get-tuple-element.28.y_last), channel_id=1, source_target_pairs={{0,1},{1,2},{2,3},{3,0},{4,5},{5,6},{6,7},{7,4},{8,9},{9,10},{10,1... | collective-permute-start | bytes 983048 | tf_op jit(solution)/shard_map/ppermute | solution.py:579
  4.4 16.2 %collective-permute-start.1 = (f32[5,32,512]{2,1,0:T(8,128)S(1)}, f32[5,32,512]{2,1,0:T(8,128)S(1)}, u32[]{:S(2)}, u32[]{:S(2)}) collective-permute-start(f32[5,32,512]{2,1,0:T(8,128)S(1)} %get-tuple-element.29.y_first), channel_id=1, source_target_pairs={{1,0},{2,1},{3,2},{0,3},{5,4},{6,5},{7,6},{4,7},{9,8},{10,9},{11,1... | collective-permute-start | bytes 983048 | tf_op jit(solution)/shard_map/ppermute | solution.py:580
  7.5 2.1 %collective-permute-start.2 = (f32[16,8,512]{2,1,0:T(8,128)S(1)}, f32[16,8,512]{2,1,0:T(8,128)S(1)}, u32[]{:S(2)}, u32[]{:S(2)}) collective-permute-start(f32[16,8,512]{2,1,0:T(8,128)S(1)} %get-tuple-element.34.own), channel_id=1, source_target_pairs={{0,4},{4,0},{8,12},{12,8},{16,20},{20,16},{24,28},{28,24},{1,5},{5... | collective-permute-start | bytes 786440 | tf_op jit(solution)/shard_map/ppermute | solution.py:568
  9.7 8.3 %collective-permute-start.5 = (f32[16,8,256]{2,1,0:T(8,128)S(1)}, f32[16,8,256]{2,1,0:T(8,128)S(1)}, u32[]{:S(2)}, u32[]{:S(2)}) collective-permute-start(f32[16,8,256]{2,1,0:T(8,128)S(1)} %get-tuple-element.35.own), channel_id=1, source_target_pairs={{0,24},{4,28},{8,16},{12,20},{16,8},{20,12},{24,0},{28,4},{1,25},{... | collective-permute-start | bytes 393224 | tf_op jit(solution)/shard_map/ppermute | solution.py:564
  12.4 7.0 %collective-permute-start.4 = (f32[16,8,256]{2,1,0:T(8,128)S(1)}, f32[16,8,256]{2,1,0:T(8,128)S(1)}, u32[]{:S(2)}, u32[]{:S(2)}) collective-permute-start(f32[16,8,256]{2,1,0:T(8,128)S(1)} %get-tuple-element.35.own), channel_id=1, source_target_pairs={{0,16},{4,20},{8,24},{12,28},{16,0},{20,4},{24,8},{28,12},{1,17},{... | collective-permute-start | bytes 393224 | tf_op jit(solution)/shard_map/ppermute | solution.py:564
  12.9 6.7 %collective-permute-start.3 = (f32[16,8,256]{2,1,0:T(8,128)S(1)}, f32[16,8,256]{2,1,0:T(8,128)S(1)}, u32[]{:S(2)}, u32[]{:S(2)}) collective-permute-start(f32[16,8,256]{2,1,0:T(8,128)S(1)} %get-tuple-element.35.own), channel_id=1, source_target_pairs={{0,8},{4,12},{8,0},{12,4},{16,24},{20,28},{24,16},{28,20},{1,9},{5... | collective-permute-start | bytes 393224 | tf_op jit(solution)/shard_map/ppermute | solution.py:564
  20.9 1.3 %collective-permute-start.6 = (f32[8,8,256]{2,1,0:T(8,128)S(1)}, f32[8,8,256]{2,1,0:T(8,128)S(1)}, u32[]{:S(2)}, u32[]{:S(2)}) collective-permute-start(f32[8,8,256]{2,1,0:T(8,128)S(1)} %get-tuple-element.38), channel_id=1, source_target_pairs={{0,4},{4,0},{8,12},{12,8},{16,20},{20,16},{24,28},{28,24},{1,5},{5... | collective-permute-start | bytes 196616 | tf_op jit(solution)/shard_map/ppermute | solution.py:568
  22.3 4.9 %collective-permute-start.9 = (f32[4,8,256]{2,1,0:T(8,128)S(1)}, f32[4,8,256]{2,1,0:T(8,128)S(1)}, u32[]{:S(2)}, u32[]{:S(2)}) collective-permute-start(f32[4,8,256]{2,1,0:T(8,128)S(1)} %get-tuple-element.46), channel_id=1, source_target_pairs={{0,24},{4,28},{8,16},{12,20},{16,8},{20,12},{24,0},{28,4},{1,25},{... | collective-permute-start | bytes 98312 | tf_op jit(solution)/shard_map/ppermute | solution.py:564
  24.8 4.5 %collective-permute-start.7 = (f32[8,8,256]{2,1,0:T(8,128)S(1)}, f32[8,8,256]{2,1,0:T(8,128)S(1)}, u32[]{:S(2)}, u32[]{:S(2)}) collective-permute-start(f32[8,8,256]{2,1,0:T(8,128)S(1)} %get-tuple-element.45.own), channel_id=1, source_target_pairs={{0,8},{4,12},{8,0},{12,4},{16,24},{20,28},{24,16},{28,20},{1,9},{5... | collective-permute-start | bytes 196616 | tf_op jit(solution)/shard_map/ppermute | solution.py:564
  25.3 3.9 %collective-permute-start.8 = (f32[4,8,256]{2,1,0:T(8,128)S(1)}, f32[4,8,256]{2,1,0:T(8,128)S(1)}, u32[]{:S(2)}, u32[]{:S(2)}) collective-permute-start(f32[4,8,256]{2,1,0:T(8,128)S(1)} %get-tuple-element.46), channel_id=1, source_target_pairs={{0,16},{4,20},{8,24},{12,28},{16,0},{20,4},{24,8},{28,12},{1,17},{... | collective-permute-start | bytes 98312 | tf_op jit(solution)/shard_map/ppermute | solution.py:564
  29.3 1.3 %collective-permute-start.10 = (f32[8,8,256]{2,1,0:T(8,128)S(1)}, f32[8,8,256]{2,1,0:T(8,128)S(1)}, u32[]{:S(2)}, u32[]{:S(2)}) collective-permute-start(f32[8,8,256]{2,1,0:T(8,128)S(1)} %get-tuple-element.49), channel_id=1, source_target_pairs={{0,4},{4,0},{8,12},{12,8},{16,20},{20,16},{24,28},{28,24},{1,5},{5... | collective-permute-start | bytes 196616 | tf_op jit(solution)/shard_map/ppermute | solution.py:568

commit v3 on v2

--- a/solution.py
+++ b/solution.py
@@ -80,8 +80,8 @@
         for k in range(4):
             copies.append(pltpu.make_async_copy(fields.at[k, :, at], out.at[k], sems.at[j, k]))
         copies.append(pltpu.make_async_copy(visc.at[:, at], out.at[4], sems.at[j, 4]))
-    for copy in copies:
-        copy.start()
+    for i, copy in enumerate(copies):
+        copy.start(priority=i % 2)
     for copy in copies:
         copy.wait()
 
@@ -540,7 +540,7 @@
                     buf.at[:, x, :, near], out.at[:, x, :, z], sems.at[c * parts + r]
                 )
             )
-            copies[-1].start()
+            copies[-1].start(priority=len(copies) % 2)
     for copy in copies:
         copy.wait()
 

time: 31.9 us -> 31.9 us (level)
  no operation moved by 1% of the time
where the time goes in v3:
time: 31.9 us; the launch traced here: 31.7 us
  Pallas kernels  12.7 us (40%)
  starting transfers between devices  12.5 us (39%)
  waiting for transfers between devices  6.38 us (20%)
    pallas_call x14, Pallas kernels, call(): pl.pallas_call(kernel, out_shape=out_shape, in_specs=in_specs, out_specs=...  12.7 us
    ppermute x6, starting transfers between devices, gather(): found[d] = lax.ppermute(x, 'line', [(i, i ^ d << 1) for i in range(lines)])  7.11 us
    ppermute x6, waiting for transfers between devices, gather(): found[d] = lax.ppermute(x, 'line', [(i, i ^ d << 1) for i in range(lines)])  5.02 us
    ppermute x1, starting transfers between devices, local(): low = lax.ppermute(y_last, 'col', ring)  3.08 us
    ppermute x1, starting transfers between devices, local(): high = lax.ppermute(y_first, 'col', back_ring)  2.09 us
    ppermute x1, waiting for transfers between devices, local(): high = lax.ppermute(y_first, 'col', back_ring)  0.9 us
  transfers between devices with their start and end apart: 11, of which 7 were waited for; matrix products, arithmetic and copies ran while one was open for 0% of the time, Pallas kernels for 31%

profile of v3, /device:TPU:0, one launch (start us, length us, event | category | flops | bytes accessed | tf_op | source)
XLA Modules:
  0.0 31.7 jit_solution(7255586299325768984)
XLA Ops:
  0.0 1.3 %cut.1 = (f32[5,32,512]{2,1,0:T(8,128)S(1)}, f32[5,32,512]{2,1,0:T(8,128)S(1)}) custom-call(f32[4,32,8,512]{3,2,1,0:T(8,128)} %fields_ref.5, f32[32,8,512]{2,1,0:T(8,128)} %visc.7), custom_call_target="tpu_custom_call" | custom-call | bytes 262144 | tf_op jit(solution)/shard_map/cut/pallas_call | solution.py:56
  1.4 3.1 %collective-permute-start = (f32[5,32,512]{2,1,0:T(8,128)S(1)}, f32[5,32,512]{2,1,0:T(8,128)S(1)}, u32[]{:S(2)}, u32[]{:S(2)}) collective-permute-start(f32[5,32,512]{2,1,0:T(8,128)S(1)} %get-tuple-element.28.y_last), channel_id=1, source_target_pairs={{0,1},{1,2},{2,3},{3,0},{4,5},{5,6},{6,7},{7,4},{8,9},{9,10},{10,1... | collective-permute-start | bytes 983048 | tf_op jit(solution)/shard_map/ppermute | solution.py:579
  4.4 2.1 %collective-permute-start.1 = (f32[5,32,512]{2,1,0:T(8,128)S(1)}, f32[5,32,512]{2,1,0:T(8,128)S(1)}, u32[]{:S(2)}, u32[]{:S(2)}) collective-permute-start(f32[5,32,512]{2,1,0:T(8,128)S(1)} %get-tuple-element.29.y_first), channel_id=1, source_target_pairs={{1,0},{2,1},{3,2},{0,3},{5,4},{6,5},{7,6},{4,7},{9,8},{10,9},{11,1... | collective-permute-start | bytes 983048 | tf_op jit(solution)/shard_map/ppermute | solution.py:580
  6.5 0.9 %factor.1 = (f32[2,32,8,512]{3,2,1,0:T(8,128)S(1)}, f32[2,32,8,512]{3,2,1,0:T(8,128)S(1)}, f32[2,32,8,512]{3,2,1,0:T(8,128)S(1)}, f32[2,32,8,512]{3,2,1,0:T(8,128)S(1)}, f32[16,8,512]{2,1,0:T(8,128)S(1)}) custom-call(f32[4,32,8,512]{3,2,1,0:T(8,128)} %fields_ref.5, f32[32,8,512]{2,1,0:T(8,128)S(1)} %copy-done), custom_call_target="tpu_custom_call" | custom-call | flops 1000000000 | tf_op jit(solution)/shard_map/factor/pallas_call | solution.py:56
  7.6 2.0 %early.1.refs_0_ = f32[4,8,8,512]{3,2,1,0:T(8,128)S(1)} custom-call(f32[4,32,8,512]{3,2,1,0:T(8,128)} %fields_ref.5, f32[32,8,512]{2,1,0:T(8,128)S(1)} %copy-done), custom_call_target="tpu_custom_call" | custom-call | flops 4000000000 | tf_op jit(solution)/shard_map/early/pallas_call | solution.py:56
  9.7 2.7 %collective-permute-start.5 = (f32[16,8,256]{2,1,0:T(8,128)S(1)}, f32[16,8,256]{2,1,0:T(8,128)S(1)}, u32[]{:S(2)}, u32[]{:S(2)}) collective-permute-start(f32[16,8,256]{2,1,0:T(8,128)S(1)} %get-tuple-element.35.own), channel_id=1, source_target_pairs={{0,24},{4,28},{8,16},{12,20},{16,8},{20,12},{24,0},{28,4},{1,25},{... | collective-permute-start | bytes 393224 | tf_op jit(solution)/shard_map/ppermute | solution.py:564
  12.4 0.5 %collective-permute-start.4 = (f32[16,8,256]{2,1,0:T(8,128)S(1)}, f32[16,8,256]{2,1,0:T(8,128)S(1)}, u32[]{:S(2)}, u32[]{:S(2)}) collective-permute-start(f32[16,8,256]{2,1,0:T(8,128)S(1)} %get-tuple-element.35.own), channel_id=1, source_target_pairs={{0,16},{4,20},{8,24},{12,28},{16,0},{20,4},{24,8},{28,12},{1,17},{... | collective-permute-start | bytes 393224 | tf_op jit(solution)/shard_map/ppermute | solution.py:564
  12.9 0.4 %collective-permute-start.3 = (f32[16,8,256]{2,1,0:T(8,128)S(1)}, f32[16,8,256]{2,1,0:T(8,128)S(1)}, u32[]{:S(2)}, u32[]{:S(2)}) collective-permute-start(f32[16,8,256]{2,1,0:T(8,128)S(1)} %get-tuple-element.35.own), channel_id=1, source_target_pairs={{0,8},{4,12},{8,0},{12,4},{16,24},{20,28},{24,16},{28,20},{1,9},{5... | collective-permute-start | bytes 393224 | tf_op jit(solution)/shard_map/ppermute | solution.py:564
  13.2 4.7 %explicit.1 = (f32[4,24,8,512]{3,2,1,0:T(8,128)S(1)}, f32[8,8,512]{2,1,0:T(8,128)S(1)}, f32[8,32,512]{2,1,0:T(8,128)S(1)}) custom-call(f32[4,32,8,512]{3,2,1,0:T(8,128)} %fields_ref.5, f32[32,8,512]{2,1,0:T(8,128)S(1)} %copy-done, f32[2,32,8,512]{3,2,1,0:T(8,128)S(1)} %get-tuple-element.30.g0, f32[2,32,8,512]{3,2,1,0:T(8,128)S(1)} %get-tuple-element.31.gn, ...), custom_call_target="tpu_custom_call" | custom-call | flops 5000000000 | tf_op jit(solution)/shard_map/explicit/pallas_call | solution.py:56
  18.0 1.4 %collective-permute-done.4.refs_1_ = f32[16,8,256]{2,1,0:T(8,128)S(1)} collective-permute-done((f32[16,8,256]{2,1,0:T(8,128)S(1)}, f32[16,8,256]{2,1,0:T(8,128)S(1)}, u32[]{:S(2)}, u32[]{:S(2)}) %collective-permute-start.4) | collective-permute-done | bytes 131104 | tf_op jit(solution)/shard_map/ppermute | solution.py:564
  19.4 0.3 collective-permute-done.3.refs_0_
  19.7 0.9 %collective-permute-done.1.high = f32[5,32,512]{2,1,0:T(8,128)S(1)} collective-permute-done((f32[5,32,512]{2,1,0:T(8,128)S(1)}, f32[5,32,512]{2,1,0:T(8,128)S(1)}, u32[]{:S(2)}, u32[]{:S(2)}) %collective-permute-start.1) | collective-permute-done | bytes 327712 | tf_op jit(solution)/shard_map/ppermute | solution.py:580
  20.6 0.3 edge.1
  21.0 0.6 %source.1.t = f32[4,32,8,512]{3,2,1,0:T(8,128)S(1)} custom-call(f32[4,8,8,512]{3,2,1,0:T(8,128)S(1)} %early.1.refs_0_, f32[4,24,8,512]{3,2,1,0:T(8,128)S(1)} %get-tuple-element.41.src, f32[2,32,8,512]{3,2,1,0:T(8,128)S(1)} %get-tuple-element.42.cpr, f32[8,32,512]{2,1,0:T(8,128)S(1)} %get-tuple-element.43.add), custom_call_target="tpu_custom_call" | custom-call | flops 3932160 | bytes 3145728 | tf_op jit(solution)/shard_map/source/pallas_call | solution.py:56
  21.6 0.4 %back.1.refs_2_.part = f32[4,32,8,512]{3,2,1,0:T(8,128)S(1)} custom-call(f32[4,32,8,512]{3,2,1,0:T(8,128)S(1)} %source.1.t, f32[2,32,8,512]{3,2,1,0:T(8,128)S(1)} %get-tuple-element.44.inv, f32[2,32,8,512]{3,2,1,0:T(8,128)S(1)} %get-tuple-element.42.cpr), custom_call_target="tpu_custom_call" | custom-call | flops 2621440 | bytes 3145728 | tf_op jit(solution)/shard_map/back/pallas_call | solution.py:56
  21.9 0.3 collective-permute-done.6.other
  22.3 2.5 %collective-permute-start.9 = (f32[4,8,256]{2,1,0:T(8,128)S(1)}, f32[4,8,256]{2,1,0:T(8,128)S(1)}, u32[]{:S(2)}, u32[]{:S(2)}) collective-permute-start(f32[4,8,256]{2,1,0:T(8,128)S(1)} %get-tuple-element.46), channel_id=1, source_target_pairs={{0,24},{4,28},{8,16},{12,20},{16,8},{20,12},{24,0},{28,4},{1,25},{... | collective-permute-start | bytes 98312 | tf_op jit(solution)/shard_map/ppermute | solution.py:564
  24.8 0.5 %collective-permute-start.7 = (f32[8,8,256]{2,1,0:T(8,128)S(1)}, f32[8,8,256]{2,1,0:T(8,128)S(1)}, u32[]{:S(2)}, u32[]{:S(2)}) collective-permute-start(f32[8,8,256]{2,1,0:T(8,128)S(1)} %get-tuple-element.45.own), channel_id=1, source_target_pairs={{0,8},{4,12},{8,0},{12,4},{16,24},{20,28},{24,16},{28,20},{1,9},{5... | collective-permute-start | bytes 196616 | tf_op jit(solution)/shard_map/ppermute | solution.py:564
  25.3 0.5 %collective-permute-start.8 = (f32[4,8,256]{2,1,0:T(8,128)S(1)}, f32[4,8,256]{2,1,0:T(8,128)S(1)}, u32[]{:S(2)}, u32[]{:S(2)}) collective-permute-start(f32[4,8,256]{2,1,0:T(8,128)S(1)} %get-tuple-element.46), channel_id=1, source_target_pairs={{0,16},{4,20},{8,24},{12,28},{16,0},{20,4},{24,8},{28,12},{1,17},{... | collective-permute-start | bytes 98312 | tf_op jit(solution)/shard_map/ppermute | solution.py:564
  25.8 1.3 %collective-permute-done.9.refs_0_ = f32[4,8,256]{2,1,0:T(8,128)S(1)} collective-permute-done((f32[4,8,256]{2,1,0:T(8,128)S(1)}, f32[4,8,256]{2,1,0:T(8,128)S(1)}, u32[]{:S(2)}, u32[]{:S(2)}) %collective-permute-start.9) | collective-permute-done | bytes 32800 | tf_op jit(solution)/shard_map/ppermute | solution.py:564
  27.2 2.1 %collective-permute-done.8.refs_1_ = f32[4,8,256]{2,1,0:T(8,128)S(1)} collective-permute-done((f32[4,8,256]{2,1,0:T(8,128)S(1)}, f32[4,8,256]{2,1,0:T(8,128)S(1)}, u32[]{:S(2)}, u32[]{:S(2)}) %collective-permute-start.8) | collective-permute-done | bytes 32800 | tf_op jit(solution)/shard_map/ppermute | solution.py:564
  29.4 1.1 %final_own.1.refs_0_ = f32[4,32,8,512]{3,2,1,0:T(8,128)} custom-call(f32[8,8,256]{2,1,0:T(8,128)S(1)} %get-tuple-element.50.flux, f32[4,32,8,512]{3,2,1,0:T(8,128)S(1)} %back.1.refs_2_.part, f32[2,32,8,512]{3,2,1,0:T(8,128)S(1)} %get-tuple-element.30.g0, f32[2,32,8,512]{3,2,1,0:T(8,128)S(1)} %get-tuple-element.31.gn), custom_call_target="tpu_custom_call" | custom-call | flops 1000000000 | tf_op jit(solution)/shard_map/final_own/pallas_call | solution.py:56
  30.5 0.2 collective-permute-done.10.flux
  30.6 1.1 %final_other.1 = f32[4,32,8,512]{3,2,1,0:T(8,128)} custom-call(f32[8,8,256]{2,1,0:T(8,128)S(1)} %collective-permute-done.10.flux, f32[4,32,8,512]{3,2,1,0:T(8,128)S(1)} %back.1.refs_2_.part, f32[2,32,8,512]{3,2,1,0:T(8,128)S(1)} %get-tuple-element.30.g0, f32[2,32,8,512]{3,2,1,0:T(8,128)S(1)} %get-tuple-element.31.gn, ...), custom_call_target="tpu_custom_call", output_to_operand_aliasing={{}: (4, {})} | custom-call | flops 1000000000 | tf_op jit(solution)/shard_map/final_other/pallas_call | solution.py:56
  (14 shorter events, 0.5 us)
Async XLA Ops:
  0.0 6.5 %copy-start = (f32[32,8,512]{2,1,0:T(8,128)S(1)}, f32[32,8,512]{2,1,0:T(8,128)}, u32[]{:S(2)}) copy-start(f32[32,8,512]{2,1,0:T(8,128)} %visc.7) | copy-start | bytes 1572868
  1.4 18.4 %collective-permute-start = (f32[5,32,512]{2,1,0:T(8,128)S(1)}, f32[5,32,512]{2,1,0:T(8,128)S(1)}, u32[]{:S(2)}, u32[]{:S(2)}) collective-permute-start(f32[5,32,512]{2,1,0:T(8,128)S(1)} %get-tuple-element.28.y_last), channel_id=1, source_target_pairs={{0,1},{1,2},{2,3},{3,0},{4,5},{5,6},{6,7},{7,4},{8,9},{9,10},{10,1... | collective-permute-start | bytes 983048 | tf_op jit(solution)/shard_map/ppermute | solution.py:579
  4.4 16.2 %collective-permute-start.1 = (f32[5,32,512]{2,1,0:T(8,128)S(1)}, f32[5,32,512]{2,1,0:T(8,128)S(1)}, u32[]{:S(2)}, u32[]{:S(2)}) collective-permute-start(f32[5,32,512]{2,1,0:T(8,128)S(1)} %get-tuple-element.29.y_first), channel_id=1, source_target_pairs={{1,0},{2,1},{3,2},{0,3},{5,4},{6,5},{7,6},{4,7},{9,8},{10,9},{11,1... | collective-permute-start | bytes 983048 | tf_op jit(solution)/shard_map/ppermute | solution.py:580
  7.5 2.1 %collective-permute-start.2 = (f32[16,8,512]{2,1,0:T(8,128)S(1)}, f32[16,8,512]{2,1,0:T(8,128)S(1)}, u32[]{:S(2)}, u32[]{:S(2)}) collective-permute-start(f32[16,8,512]{2,1,0:T(8,128)S(1)} %get-tuple-element.34.own), channel_id=1, source_target_pairs={{0,4},{4,0},{8,12},{12,8},{16,20},{20,16},{24,28},{28,24},{1,5},{5... | collective-permute-start | bytes 786440 | tf_op jit(solution)/shard_map/ppermute | solution.py:568
  9.7 8.3 %collective-permute-start.5 = (f32[16,8,256]{2,1,0:T(8,128)S(1)}, f32[16,8,256]{2,1,0:T(8,128)S(1)}, u32[]{:S(2)}, u32[]{:S(2)}) collective-permute-start(f32[16,8,256]{2,1,0:T(8,128)S(1)} %get-tuple-element.35.own), channel_id=1, source_target_pairs={{0,24},{4,28},{8,16},{12,20},{16,8},{20,12},{24,0},{28,4},{1,25},{... | collective-permute-start | bytes 393224 | tf_op jit(solution)/shard_map/ppermute | solution.py:564
  12.4 7.0 %collective-permute-start.4 = (f32[16,8,256]{2,1,0:T(8,128)S(1)}, f32[16,8,256]{2,1,0:T(8,128)S(1)}, u32[]{:S(2)}, u32[]{:S(2)}) collective-permute-start(f32[16,8,256]{2,1,0:T(8,128)S(1)} %get-tuple-element.35.own), channel_id=1, source_target_pairs={{0,16},{4,20},{8,24},{12,28},{16,0},{20,4},{24,8},{28,12},{1,17},{... | collective-permute-start | bytes 393224 | tf_op jit(solution)/shard_map/ppermute | solution.py:564
  12.9 6.7 %collective-permute-start.3 = (f32[16,8,256]{2,1,0:T(8,128)S(1)}, f32[16,8,256]{2,1,0:T(8,128)S(1)}, u32[]{:S(2)}, u32[]{:S(2)}) collective-permute-start(f32[16,8,256]{2,1,0:T(8,128)S(1)} %get-tuple-element.35.own), channel_id=1, source_target_pairs={{0,8},{4,12},{8,0},{12,4},{16,24},{20,28},{24,16},{28,20},{1,9},{5... | collective-permute-start | bytes 393224 | tf_op jit(solution)/shard_map/ppermute | solution.py:564
  20.9 1.3 %collective-permute-start.6 = (f32[8,8,256]{2,1,0:T(8,128)S(1)}, f32[8,8,256]{2,1,0:T(8,128)S(1)}, u32[]{:S(2)}, u32[]{:S(2)}) collective-permute-start(f32[8,8,256]{2,1,0:T(8,128)S(1)} %get-tuple-element.38), channel_id=1, source_target_pairs={{0,4},{4,0},{8,12},{12,8},{16,20},{20,16},{24,28},{28,24},{1,5},{5... | collective-permute-start | bytes 196616 | tf_op jit(solution)/shard_map/ppermute | solution.py:568
  22.3 4.9 %collective-permute-start.9 = (f32[4,8,256]{2,1,0:T(8,128)S(1)}, f32[4,8,256]{2,1,0:T(8,128)S(1)}, u32[]{:S(2)}, u32[]{:S(2)}) collective-permute-start(f32[4,8,256]{2,1,0:T(8,128)S(1)} %get-tuple-element.46), channel_id=1, source_target_pairs={{0,24},{4,28},{8,16},{12,20},{16,8},{20,12},{24,0},{28,4},{1,25},{... | collective-permute-start | bytes 98312 | tf_op jit(solution)/shard_map/ppermute | solution.py:564
  24.8 4.5 %collective-permute-start.7 = (f32[8,8,256]{2,1,0:T(8,128)S(1)}, f32[8,8,256]{2,1,0:T(8,128)S(1)}, u32[]{:S(2)}, u32[]{:S(2)}) collective-permute-start(f32[8,8,256]{2,1,0:T(8,128)S(1)} %get-tuple-element.45.own), channel_id=1, source_target_pairs={{0,8},{4,12},{8,0},{12,4},{16,24},{20,28},{24,16},{28,20},{1,9},{5... | collective-permute-start | bytes 196616 | tf_op jit(solution)/shard_map/ppermute | solution.py:564
  25.3 3.9 %collective-permute-start.8 = (f32[4,8,256]{2,1,0:T(8,128)S(1)}, f32[4,8,256]{2,1,0:T(8,128)S(1)}, u32[]{:S(2)}, u32[]{:S(2)}) collective-permute-start(f32[4,8,256]{2,1,0:T(8,128)S(1)} %get-tuple-element.46), channel_id=1, source_target_pairs={{0,16},{4,20},{8,24},{12,28},{16,0},{20,4},{24,8},{28,12},{1,17},{... | collective-permute-start | bytes 98312 | tf_op jit(solution)/shard_map/ppermute | solution.py:564
  29.3 1.3 %collective-permute-start.10 = (f32[8,8,256]{2,1,0:T(8,128)S(1)}, f32[8,8,256]{2,1,0:T(8,128)S(1)}, u32[]{:S(2)}, u32[]{:S(2)}) collective-permute-start(f32[8,8,256]{2,1,0:T(8,128)S(1)} %get-tuple-element.49), channel_id=1, source_target_pairs={{0,4},{4,0},{8,12},{12,8},{16,20},{20,16},{24,28},{28,24},{1,5},{5... | collective-permute-start | bytes 196616 | tf_op jit(solution)/shard_map/ppermute | solution.py:568

commit v4 on v2

--- a/solution.py
+++ b/solution.py
@@ -77,9 +77,8 @@
 def cut_kernel(ny, fields, visc, y_first, y_last, sems):
     copies = []
     for j, (at, out) in enumerate(((0, y_first), (ny - 1, y_last))):
-        for k in range(4):
-            copies.append(pltpu.make_async_copy(fields.at[k, :, at], out.at[k], sems.at[j, k]))
-        copies.append(pltpu.make_async_copy(visc.at[:, at], out.at[4], sems.at[j, 4]))
+        copies.append(pltpu.make_async_copy(fields.at[:, :, at], out.at[0:4], sems.at[j, 0]))
+        copies.append(pltpu.make_async_copy(visc.at[:, at], out.at[4], sems.at[j, 1]))
     for copy in copies:
         copy.start()
     for copy in copies:
@@ -572,7 +571,7 @@
         "cut",
         [(5, rows, nz), (5, rows, nz)],
         [fields, viscosity],
-        scratch=[pltpu.SemaphoreType.DMA((2, 5))],
+        scratch=[pltpu.SemaphoreType.DMA((2, 2))],
         in_hbm=(0, 1),
         moved=2 * cells,
     )

time: 31.9 us -> 31.8 us (level)
  no operation moved by 1% of the time
where the time goes in v4:
time: 31.8 us; the launch traced here: 31.6 us
  Pallas kernels  12.5 us (39%)
  starting transfers between devices  12.5 us (39%)
  waiting for transfers between devices  6.38 us (20%)
    pallas_call x14, Pallas kernels, call(): pl.pallas_call(kernel, out_shape=out_shape, in_specs=in_specs, out_specs=...  12.5 us
    ppermute x6, starting transfers between devices, gather(): found[d] = lax.ppermute(x, 'line', [(i, i ^ d << 1) for i in range(lines)])  7.11 us
    ppermute x6, waiting for transfers between devices, gather(): found[d] = lax.ppermute(x, 'line', [(i, i ^ d << 1) for i in range(lines)])  5.02 us
    ppermute x1, starting transfers between devices, local(): low = lax.ppermute(y_last, 'col', ring)  3.08 us
    ppermute x1, starting transfers between devices, local(): high = lax.ppermute(y_first, 'col', back_ring)  2.09 us
    ppermute x1, waiting for transfers between devices, local(): high = lax.ppermute(y_first, 'col', back_ring)  0.9 us
  transfers between devices with their start and end apart: 11, of which 7 were waited for; matrix products, arithmetic and copies ran while one was open for 0% of the time, Pallas kernels for 31%

profile of v4, /device:TPU:0, one launch (start us, length us, event | category | flops | bytes accessed | tf_op | source)
XLA Modules:
  0.0 31.6 jit_solution(9958909115124165820)
XLA Ops:
  0.0 1.2 %cut.1 = (f32[5,32,512]{2,1,0:T(8,128)S(1)}, f32[5,32,512]{2,1,0:T(8,128)S(1)}) custom-call(f32[4,32,8,512]{3,2,1,0:T(8,128)} %fields_ref.5, f32[32,8,512]{2,1,0:T(8,128)} %visc.7), custom_call_target="tpu_custom_call" | custom-call | bytes 262144 | tf_op jit(solution)/shard_map/cut/pallas_call | solution.py:56
  1.2 3.1 %collective-permute-start = (f32[5,32,512]{2,1,0:T(8,128)S(1)}, f32[5,32,512]{2,1,0:T(8,128)S(1)}, u32[]{:S(2)}, u32[]{:S(2)}) collective-permute-start(f32[5,32,512]{2,1,0:T(8,128)S(1)} %get-tuple-element.28.y_last), channel_id=1, source_target_pairs={{0,1},{1,2},{2,3},{3,0},{4,5},{5,6},{6,7},{7,4},{8,9},{9,10},{10,1... | collective-permute-start | bytes 983048 | tf_op jit(solution)/shard_map/ppermute | solution.py:578
  4.3 2.1 %collective-permute-start.1 = (f32[5,32,512]{2,1,0:T(8,128)S(1)}, f32[5,32,512]{2,1,0:T(8,128)S(1)}, u32[]{:S(2)}, u32[]{:S(2)}) collective-permute-start(f32[5,32,512]{2,1,0:T(8,128)S(1)} %get-tuple-element.29.y_first), channel_id=1, source_target_pairs={{1,0},{2,1},{3,2},{0,3},{5,4},{6,5},{7,6},{4,7},{9,8},{10,9},{11,1... | collective-permute-start | bytes 983048 | tf_op jit(solution)/shard_map/ppermute | solution.py:579
  6.4 0.9 %factor.1 = (f32[2,32,8,512]{3,2,1,0:T(8,128)S(1)}, f32[2,32,8,512]{3,2,1,0:T(8,128)S(1)}, f32[2,32,8,512]{3,2,1,0:T(8,128)S(1)}, f32[2,32,8,512]{3,2,1,0:T(8,128)S(1)}, f32[16,8,512]{2,1,0:T(8,128)S(1)}) custom-call(f32[4,32,8,512]{3,2,1,0:T(8,128)} %fields_ref.5, f32[32,8,512]{2,1,0:T(8,128)S(1)} %copy-done), custom_call_target="tpu_custom_call" | custom-call | flops 1000000000 | tf_op jit(solution)/shard_map/factor/pallas_call | solution.py:56
  7.4 2.0 %early.1.refs_0_ = f32[4,8,8,512]{3,2,1,0:T(8,128)S(1)} custom-call(f32[4,32,8,512]{3,2,1,0:T(8,128)} %fields_ref.5, f32[32,8,512]{2,1,0:T(8,128)S(1)} %copy-done), custom_call_target="tpu_custom_call" | custom-call | flops 4000000000 | tf_op jit(solution)/shard_map/early/pallas_call | solution.py:56
  9.6 2.7 %collective-permute-start.5 = (f32[16,8,256]{2,1,0:T(8,128)S(1)}, f32[16,8,256]{2,1,0:T(8,128)S(1)}, u32[]{:S(2)}, u32[]{:S(2)}) collective-permute-start(f32[16,8,256]{2,1,0:T(8,128)S(1)} %get-tuple-element.35.own), channel_id=1, source_target_pairs={{0,24},{4,28},{8,16},{12,20},{16,8},{20,12},{24,0},{28,4},{1,25},{... | collective-permute-start | bytes 393224 | tf_op jit(solution)/shard_map/ppermute | solution.py:563
  12.2 0.5 %collective-permute-start.4 = (f32[16,8,256]{2,1,0:T(8,128)S(1)}, f32[16,8,256]{2,1,0:T(8,128)S(1)}, u32[]{:S(2)}, u32[]{:S(2)}) collective-permute-start(f32[16,8,256]{2,1,0:T(8,128)S(1)} %get-tuple-element.35.own), channel_id=1, source_target_pairs={{0,16},{4,20},{8,24},{12,28},{16,0},{20,4},{24,8},{28,12},{1,17},{... | collective-permute-start | bytes 393224 | tf_op jit(solution)/shard_map/ppermute | solution.py:563
  12.7 0.4 %collective-permute-start.3 = (f32[16,8,256]{2,1,0:T(8,128)S(1)}, f32[16,8,256]{2,1,0:T(8,128)S(1)}, u32[]{:S(2)}, u32[]{:S(2)}) collective-permute-start(f32[16,8,256]{2,1,0:T(8,128)S(1)} %get-tuple-element.35.own), channel_id=1, source_target_pairs={{0,8},{4,12},{8,0},{12,4},{16,24},{20,28},{24,16},{28,20},{1,9},{5... | collective-permute-start | bytes 393224 | tf_op jit(solution)/shard_map/ppermute | solution.py:563
  13.1 4.7 %explicit.1 = (f32[4,24,8,512]{3,2,1,0:T(8,128)S(1)}, f32[8,8,512]{2,1,0:T(8,128)S(1)}, f32[8,32,512]{2,1,0:T(8,128)S(1)}) custom-call(f32[4,32,8,512]{3,2,1,0:T(8,128)} %fields_ref.5, f32[32,8,512]{2,1,0:T(8,128)S(1)} %copy-done, f32[2,32,8,512]{3,2,1,0:T(8,128)S(1)} %get-tuple-element.30.g0, f32[2,32,8,512]{3,2,1,0:T(8,128)S(1)} %get-tuple-element.31.gn, ...), custom_call_target="tpu_custom_call" | custom-call | flops 5000000000 | tf_op jit(solution)/shard_map/explicit/pallas_call | solution.py:56
  17.9 1.4 %collective-permute-done.4.refs_1_ = f32[16,8,256]{2,1,0:T(8,128)S(1)} collective-permute-done((f32[16,8,256]{2,1,0:T(8,128)S(1)}, f32[16,8,256]{2,1,0:T(8,128)S(1)}, u32[]{:S(2)}, u32[]{:S(2)}) %collective-permute-start.4) | collective-permute-done | bytes 131104 | tf_op jit(solution)/shard_map/ppermute | solution.py:563
  19.2 0.3 collective-permute-done.3.refs_0_
  19.6 0.9 %collective-permute-done.1.high = f32[5,32,512]{2,1,0:T(8,128)S(1)} collective-permute-done((f32[5,32,512]{2,1,0:T(8,128)S(1)}, f32[5,32,512]{2,1,0:T(8,128)S(1)}, u32[]{:S(2)}, u32[]{:S(2)}) %collective-permute-start.1) | collective-permute-done | bytes 327712 | tf_op jit(solution)/shard_map/ppermute | solution.py:579
  20.5 0.3 edge.1
  20.9 0.6 %source.1.t = f32[4,32,8,512]{3,2,1,0:T(8,128)S(1)} custom-call(f32[4,8,8,512]{3,2,1,0:T(8,128)S(1)} %early.1.refs_0_, f32[4,24,8,512]{3,2,1,0:T(8,128)S(1)} %get-tuple-element.41.src, f32[2,32,8,512]{3,2,1,0:T(8,128)S(1)} %get-tuple-element.42.cpr, f32[8,32,512]{2,1,0:T(8,128)S(1)} %get-tuple-element.43.add), custom_call_target="tpu_custom_call" | custom-call | flops 3932160 | bytes 3145728 | tf_op jit(solution)/shard_map/source/pallas_call | solution.py:56
  21.4 0.4 %back.1.refs_2_.part = f32[4,32,8,512]{3,2,1,0:T(8,128)S(1)} custom-call(f32[4,32,8,512]{3,2,1,0:T(8,128)S(1)} %source.1.t, f32[2,32,8,512]{3,2,1,0:T(8,128)S(1)} %get-tuple-element.44.inv, f32[2,32,8,512]{3,2,1,0:T(8,128)S(1)} %get-tuple-element.42.cpr), custom_call_target="tpu_custom_call" | custom-call | flops 2621440 | bytes 3145728 | tf_op jit(solution)/shard_map/back/pallas_call | solution.py:56
  21.8 0.3 collective-permute-done.6.other
  22.1 2.5 %collective-permute-start.9 = (f32[4,8,256]{2,1,0:T(8,128)S(1)}, f32[4,8,256]{2,1,0:T(8,128)S(1)}, u32[]{:S(2)}, u32[]{:S(2)}) collective-permute-start(f32[4,8,256]{2,1,0:T(8,128)S(1)} %get-tuple-element.46), channel_id=1, source_target_pairs={{0,24},{4,28},{8,16},{12,20},{16,8},{20,12},{24,0},{28,4},{1,25},{... | collective-permute-start | bytes 98312 | tf_op jit(solution)/shard_map/ppermute | solution.py:563
  24.6 0.5 %collective-permute-start.7 = (f32[8,8,256]{2,1,0:T(8,128)S(1)}, f32[8,8,256]{2,1,0:T(8,128)S(1)}, u32[]{:S(2)}, u32[]{:S(2)}) collective-permute-start(f32[8,8,256]{2,1,0:T(8,128)S(1)} %get-tuple-element.45.own), channel_id=1, source_target_pairs={{0,8},{4,12},{8,0},{12,4},{16,24},{20,28},{24,16},{28,20},{1,9},{5... | collective-permute-start | bytes 196616 | tf_op jit(solution)/shard_map/ppermute | solution.py:563
  25.2 0.5 %collective-permute-start.8 = (f32[4,8,256]{2,1,0:T(8,128)S(1)}, f32[4,8,256]{2,1,0:T(8,128)S(1)}, u32[]{:S(2)}, u32[]{:S(2)}) collective-permute-start(f32[4,8,256]{2,1,0:T(8,128)S(1)} %get-tuple-element.46), channel_id=1, source_target_pairs={{0,16},{4,20},{8,24},{12,28},{16,0},{20,4},{24,8},{28,12},{1,17},{... | collective-permute-start | bytes 98312 | tf_op jit(solution)/shard_map/ppermute | solution.py:563
  25.7 1.3 %collective-permute-done.9.refs_0_ = f32[4,8,256]{2,1,0:T(8,128)S(1)} collective-permute-done((f32[4,8,256]{2,1,0:T(8,128)S(1)}, f32[4,8,256]{2,1,0:T(8,128)S(1)}, u32[]{:S(2)}, u32[]{:S(2)}) %collective-permute-start.9) | collective-permute-done | bytes 32800 | tf_op jit(solution)/shard_map/ppermute | solution.py:563
  27.0 2.1 %collective-permute-done.8.refs_1_ = f32[4,8,256]{2,1,0:T(8,128)S(1)} collective-permute-done((f32[4,8,256]{2,1,0:T(8,128)S(1)}, f32[4,8,256]{2,1,0:T(8,128)S(1)}, u32[]{:S(2)}, u32[]{:S(2)}) %collective-permute-start.8) | collective-permute-done | bytes 32800 | tf_op jit(solution)/shard_map/ppermute | solution.py:563
  29.3 1.1 %final_own.1.refs_0_ = f32[4,32,8,512]{3,2,1,0:T(8,128)} custom-call(f32[8,8,256]{2,1,0:T(8,128)S(1)} %get-tuple-element.50.flux, f32[4,32,8,512]{3,2,1,0:T(8,128)S(1)} %back.1.refs_2_.part, f32[2,32,8,512]{3,2,1,0:T(8,128)S(1)} %get-tuple-element.30.g0, f32[2,32,8,512]{3,2,1,0:T(8,128)S(1)} %get-tuple-element.31.gn), custom_call_target="tpu_custom_call" | custom-call | flops 1000000000 | tf_op jit(solution)/shard_map/final_own/pallas_call | solution.py:56
  30.3 0.2 collective-permute-done.10.flux
  30.5 1.1 %final_other.1 = f32[4,32,8,512]{3,2,1,0:T(8,128)} custom-call(f32[8,8,256]{2,1,0:T(8,128)S(1)} %collective-permute-done.10.flux, f32[4,32,8,512]{3,2,1,0:T(8,128)S(1)} %back.1.refs_2_.part, f32[2,32,8,512]{3,2,1,0:T(8,128)S(1)} %get-tuple-element.30.g0, f32[2,32,8,512]{3,2,1,0:T(8,128)S(1)} %get-tuple-element.31.gn, ...), custom_call_target="tpu_custom_call", output_to_operand_aliasing={{}: (4, {})} | custom-call | flops 1000000000 | tf_op jit(solution)/shard_map/final_other/pallas_call | solution.py:56
  (14 shorter events, 0.5 us)
Async XLA Ops:
  0.0 6.4 %copy-start = (f32[32,8,512]{2,1,0:T(8,128)S(1)}, f32[32,8,512]{2,1,0:T(8,128)}, u32[]{:S(2)}) copy-start(f32[32,8,512]{2,1,0:T(8,128)} %visc.7) | copy-start | bytes 1572868
  1.2 18.4 %collective-permute-start = (f32[5,32,512]{2,1,0:T(8,128)S(1)}, f32[5,32,512]{2,1,0:T(8,128)S(1)}, u32[]{:S(2)}, u32[]{:S(2)}) collective-permute-start(f32[5,32,512]{2,1,0:T(8,128)S(1)} %get-tuple-element.28.y_last), channel_id=1, source_target_pairs={{0,1},{1,2},{2,3},{3,0},{4,5},{5,6},{6,7},{7,4},{8,9},{9,10},{10,1... | collective-permute-start | bytes 983048 | tf_op jit(solution)/shard_map/ppermute | solution.py:578
  4.3 16.2 %collective-permute-start.1 = (f32[5,32,512]{2,1,0:T(8,128)S(1)}, f32[5,32,512]{2,1,0:T(8,128)S(1)}, u32[]{:S(2)}, u32[]{:S(2)}) collective-permute-start(f32[5,32,512]{2,1,0:T(8,128)S(1)} %get-tuple-element.29.y_first), channel_id=1, source_target_pairs={{1,0},{2,1},{3,2},{0,3},{5,4},{6,5},{7,6},{4,7},{9,8},{10,9},{11,1... | collective-permute-start | bytes 983048 | tf_op jit(solution)/shard_map/ppermute | solution.py:579
  7.3 2.1 %collective-permute-start.2 = (f32[16,8,512]{2,1,0:T(8,128)S(1)}, f32[16,8,512]{2,1,0:T(8,128)S(1)}, u32[]{:S(2)}, u32[]{:S(2)}) collective-permute-start(f32[16,8,512]{2,1,0:T(8,128)S(1)} %get-tuple-element.34.own), channel_id=1, source_target_pairs={{0,4},{4,0},{8,12},{12,8},{16,20},{20,16},{24,28},{28,24},{1,5},{5... | collective-permute-start | bytes 786440 | tf_op jit(solution)/shard_map/ppermute | solution.py:567
  9.6 8.3 %collective-permute-start.5 = (f32[16,8,256]{2,1,0:T(8,128)S(1)}, f32[16,8,256]{2,1,0:T(8,128)S(1)}, u32[]{:S(2)}, u32[]{:S(2)}) collective-permute-start(f32[16,8,256]{2,1,0:T(8,128)S(1)} %get-tuple-element.35.own), channel_id=1, source_target_pairs={{0,24},{4,28},{8,16},{12,20},{16,8},{20,12},{24,0},{28,4},{1,25},{... | collective-permute-start | bytes 393224 | tf_op jit(solution)/shard_map/ppermute | solution.py:563
  12.2 7.0 %collective-permute-start.4 = (f32[16,8,256]{2,1,0:T(8,128)S(1)}, f32[16,8,256]{2,1,0:T(8,128)S(1)}, u32[]{:S(2)}, u32[]{:S(2)}) collective-permute-start(f32[16,8,256]{2,1,0:T(8,128)S(1)} %get-tuple-element.35.own), channel_id=1, source_target_pairs={{0,16},{4,20},{8,24},{12,28},{16,0},{20,4},{24,8},{28,12},{1,17},{... | collective-permute-start | bytes 393224 | tf_op jit(solution)/shard_map/ppermute | solution.py:563
  12.7 6.7 %collective-permute-start.3 = (f32[16,8,256]{2,1,0:T(8,128)S(1)}, f32[16,8,256]{2,1,0:T(8,128)S(1)}, u32[]{:S(2)}, u32[]{:S(2)}) collective-permute-start(f32[16,8,256]{2,1,0:T(8,128)S(1)} %get-tuple-element.35.own), channel_id=1, source_target_pairs={{0,8},{4,12},{8,0},{12,4},{16,24},{20,28},{24,16},{28,20},{1,9},{5... | collective-permute-start | bytes 393224 | tf_op jit(solution)/shard_map/ppermute | solution.py:563
  20.8 1.3 %collective-permute-start.6 = (f32[8,8,256]{2,1,0:T(8,128)S(1)}, f32[8,8,256]{2,1,0:T(8,128)S(1)}, u32[]{:S(2)}, u32[]{:S(2)}) collective-permute-start(f32[8,8,256]{2,1,0:T(8,128)S(1)} %get-tuple-element.38), channel_id=1, source_target_pairs={{0,4},{4,0},{8,12},{12,8},{16,20},{20,16},{24,28},{28,24},{1,5},{5... | collective-permute-start | bytes 196616 | tf_op jit(solution)/shard_map/ppermute | solution.py:567
  22.1 4.9 %collective-permute-start.9 = (f32[4,8,256]{2,1,0:T(8,128)S(1)}, f32[4,8,256]{2,1,0:T(8,128)S(1)}, u32[]{:S(2)}, u32[]{:S(2)}) collective-permute-start(f32[4,8,256]{2,1,0:T(8,128)S(1)} %get-tuple-element.46), channel_id=1, source_target_pairs={{0,24},{4,28},{8,16},{12,20},{16,8},{20,12},{24,0},{28,4},{1,25},{... | collective-permute-start | bytes 98312 | tf_op jit(solution)/shard_map/ppermute | solution.py:563
  24.6 4.5 %collective-permute-start.7 = (f32[8,8,256]{2,1,0:T(8,128)S(1)}, f32[8,8,256]{2,1,0:T(8,128)S(1)}, u32[]{:S(2)}, u32[]{:S(2)}) collective-permute-start(f32[8,8,256]{2,1,0:T(8,128)S(1)} %get-tuple-element.45.own), channel_id=1, source_target_pairs={{0,8},{4,12},{8,0},{12,4},{16,24},{20,28},{24,16},{28,20},{1,9},{5... | collective-permute-start | bytes 196616 | tf_op jit(solution)/shard_map/ppermute | solution.py:563
  25.2 3.9 %collective-permute-start.8 = (f32[4,8,256]{2,1,0:T(8,128)S(1)}, f32[4,8,256]{2,1,0:T(8,128)S(1)}, u32[]{:S(2)}, u32[]{:S(2)}) collective-permute-start(f32[4,8,256]{2,1,0:T(8,128)S(1)} %get-tuple-element.46), channel_id=1, source_target_pairs={{0,16},{4,20},{8,24},{12,28},{16,0},{20,4},{24,8},{28,12},{1,17},{... | collective-permute-start | bytes 98312 | tf_op jit(solution)/shard_map/ppermute | solution.py:563
  29.2 1.3 %collective-permute-start.10 = (f32[8,8,256]{2,1,0:T(8,128)S(1)}, f32[8,8,256]{2,1,0:T(8,128)S(1)}, u32[]{:S(2)}, u32[]{:S(2)}) collective-permute-start(f32[8,8,256]{2,1,0:T(8,128)S(1)} %get-tuple-element.49), channel_id=1, source_target_pairs={{0,4},{4,0},{8,12},{12,8},{16,20},{20,16},{24,28},{28,24},{1,5},{5... | collective-permute-start | bytes 196616 | tf_op jit(solution)/shard_map/ppermute | solution.py:567
